TPU v7x, 32 devices: a whole 2x2x4 slice. The times are simulated.
32 devices in a mesh: blk: 2 (over x), theta: 4 (over z), radial: 4 (over y, core).
Axes of the slice: x: 2, y: 2, z: 4, core: 2. Of those that a mesh axis runs over, the one named last changes fastest.
Arguments:
- base_state: float32 [5, 12, 32, 4096], P(None, 'blk', 'radial', 'theta'), may hold values from -4 to 12, as said below
- section_state: float32 [5, 12, 32, 4096], P(None, 'blk', 'radial', 'theta'), may hold values from -4 to 12, as said below
- rotor_step: int32 [1], replicated, may hold values from 4096 to 16383
Outputs:
- next_state: float32 [5, 12, 32, 4096], P(None, 'blk', 'radial', 'theta')
Inputs may be any that keep to these rules, and one draw needn't show every extreme that they name: `base_state`: density between 0.5 and 2, pressure between 0.5 and 2, every velocity component under 2 in magnitude. `section_state`: density between 0.5 and 2, pressure between 0.5 and 2, every velocity component under 2 in magnitude.
All inputs are finite; a program needn't handle non-finite values.
Results may differ from a plain program's by a relative error of at most 0.0003.
Values sent between devices are 32-bit elements; how exact they have to be, the bound alone decides.
No kernel may reach another device: no remote copies, remote signals or barrier semaphores. Data moves between devices by JAX's collectives and lax.ppermute only.
A program may use at most 64 MiB of HBM per device.

v0:
```python
import functools

import jax
import jax.numpy as jnp
import numpy as np
from jax import lax
from jax.experimental import pallas as pl
from jax.experimental.pallas import tpu as pltpu
from jax.sharding import PartitionSpec as P

gamma_ratio = 1.4
weno_epsilon = 1e-06
step_ratio = 0.12
lanes = 128
ghosts = 3
group = 16
flux_scale = 12.0
chunk = 512
most_slabs = 8
vmem_bytes = 48 * 1024 * 1024

axial_order = (0, 1, 2, 3, 4)
radial_order = (0, 3, 1, 2, 4)
theta_order = (0, 2, 1, 3, 4)


def inverse(value):
    guess = pl.reciprocal(value, approx=True)
    return guess * (2.0 - value * guess)


def cell_terms(state):
    density, normal, first, second, energy = state
    inv = inverse(density)
    speed = normal * inv
    kinetic = 0.5 * (normal * normal + first * first + second * second) * inv
    pressure = (gamma_ratio - 1.0) * (energy - kinetic)
    square = gamma_ratio * pressure * inv
    wave = jnp.abs(speed) + square * lax.rsqrt(square)
    flux = (normal, normal * speed + pressure, first * speed, second * speed, (energy + pressure) * speed)
    return flux, wave


def interface_terms(left, right):
    (state_l, flux_l, wave_l), (state_r, flux_r, wave_r) = left, right
    return (
        [r - l for l, r in zip(state_l, state_r)]
        + [r - l for l, r in zip(flux_l, flux_r)]
        + [0.5 * flux_scale * (r + l) for l, r in zip(flux_l, flux_r)]
        + [jnp.maximum(wave_l, wave_r)]
    )


def weno_terms(d0, d1, d2, d3, epsilon):
    e0 = d1 - d0
    e1 = d2 - d1
    e2 = d3 - d2
    f0 = e0 - e1
    f1 = e1 - e2
    t1 = 0.75 * d1
    t2 = 0.75 * d2
    shared = t1 * d2 + epsilon
    low = e0 * e0 + (t1 * f0 + shared)
    mid = e1 * e1 + shared
    high = e2 * e2 + (t2 * f1 + shared)
    x = mid * pl.reciprocal(low, approx=True)
    y = mid * pl.reciprocal(high, approx=True)
    weight_low = x * x
    weight_high = 1.5 * (y * y)
    total = 0.5 * weight_low + (weight_high + 3.0)
    return (weight_low * f0 + weight_high * f1) * pl.reciprocal(total, approx=True)


def face_terms(diff_state, diff_flux, sum_state, sum_flux, wave):
    inv = inverse(sum_state(0))
    un, va, vb, specific = (inv * sum_state(k) for k in range(1, 5))
    half = 0.5 * (un * un + va * va + vb * vb)
    internal = specific - half
    square = gamma_ratio * (gamma_ratio - 1.0) * internal
    inv_sound = lax.rsqrt(square)
    sound = square * inv_sound
    factor = (gamma_ratio - 1.0) * inv_sound * inv_sound
    enthalpy = specific + (gamma_ratio - 1.0) * internal

    def project(dens, norm, first, second, energy):
        sn = norm - un * dens
        sa = first - va * dens
        sb = second - vb * dens
        even = factor * (energy - half * dens - un * sn - va * sa - vb * sb)
        odd = inv_sound * sn
        return even - odd, dens - even, sa, sb, even + odd

    def side(vectors):
        chars = [project(*vector) for vector in vectors]
        return [weno_terms(*(c[k] for c in chars), weno_epsilon * (12.0 if k in (0, 4) else 3.0)) for k in range(5)]

    plus = [[diff_flux[s](c) + wave * diff_state[s](c) for c in range(5)] for s in range(4)]
    forward = side(plus)
    minus = [[diff_flux[s](c) - wave * diff_state[s](c) for c in range(5)] for s in range(4, 0, -1)]
    backward = side(minus)
    central = [sum_flux(c) + (plus[1][c] - plus[2][c]) + (minus[2][c] - minus[1][c]) for c in range(5)]
    wave_minus, entropy, sa, sb, wave_plus = (f - b for f, b in zip(forward, backward))
    even = 0.5 * (wave_plus + wave_minus)
    odd = sound * (0.5 * (wave_plus - wave_minus))
    carried = even + entropy
    return (
        central[0] + carried,
        central[1] + un * carried + odd,
        central[2] + va * carried + sa,
        central[3] + vb * carried + sb,
        central[4] + enthalpy * even + un * odd + half * entropy + va * sa + vb * sb,
    )


def face_from(load, sum_state):
    return face_terms(
        [functools.partial(lambda s, c: load(c, s), s) for s in range(5)],
        [functools.partial(lambda s, c: load(5 + c, s), s) for s in range(5)],
        sum_state,
        lambda c: load(10 + c, 2),
        load(15, 2),
    )


def with_terms(state):
    return (state, *cell_terms(state))


def lane_index(shape):
    return lax.broadcasted_iota(jnp.int32, shape, len(shape) - 1)


def pack_kernel(ids, section, theta_low, theta_high, theta_own, radial_low, radial_high, near, far, rows):
    planes, bands, width = section.shape[1:]
    tiles = width // lanes
    facing = jnp.where(ids[0] == 0, planes - ghosts, 0)
    for c in range(5):
        for i in range(ghosts):
            near[c, i] = section[c, facing + i, :, width - near.shape[3] :]
            far[c, i] = section[c, facing + i, :, : far.shape[3]]
    lane = lane_index((bands, lanes))
    for c in range(5):
        own = jnp.full((bands, lanes), (1.0, 0.0, 0.0, 0.0, 3.0)[c], jnp.float32)
        low = high = own
        for p in range(planes):
            at = lane - group * p
            head = section[c, p, :, 0:lanes]
            tail = section[c, p, :, width - lanes : width]
            turned_head = pltpu.roll(head, group * p + ghosts, 1)
            turned_tail = pltpu.roll(tail, group * p + group - ghosts, 1)
            own = jnp.where((at >= ghosts) & (at < group // 2), turned_head, own)
            own = jnp.where((at >= group // 2) & (at < group - ghosts), turned_tail, own)
            low = jnp.where((at >= group - ghosts) & (at < group), pltpu.roll(head, group * p + group - ghosts, 1), low)
            high = jnp.where((at >= 0) & (at < ghosts), pltpu.roll(tail, group * p + ghosts, 1), high)
        theta_own[c] = own
        theta_low[c] = low
        theta_high[c] = high
    for c in range(5):

        def plane(p, carry):
            for j in range(tiles):
                rows[j * bands : (j + 1) * bands] = section[c, p, :, j * lanes : (j + 1) * lanes]
            for k in range(ghosts):
                radial_low[c, p, k] = rows[pl.ds(k, tiles, stride=bands)]
                radial_high[c, p, k] = rows[pl.ds(bands - ghosts + k, tiles, stride=bands)]
            return carry

        lax.fori_loop(0, planes, plane, 0)


def pack(ids, section, near, far):
    _, planes, bands, width = section.shape
    tiles = width // lanes
    vmem = pl.BlockSpec(memory_space=pltpu.VMEM)
    array = lambda *shape: jax.ShapeDtypeStruct(shape, jnp.float32)
    theta = array(5, bands, lanes)
    radial = array(5, planes, ghosts, tiles, lanes)
    mortar = [array(5, ghosts, bands, part) for part in (near, far)]
    return pl.pallas_call(
        pack_kernel,
        in_specs=[pl.BlockSpec(memory_space=pltpu.SMEM), vmem],
        out_shape=(theta, theta, theta, radial, radial, *mortar),
        scratch_shapes=[pltpu.VMEM((bands * tiles, lanes), jnp.float32)],
        compiler_params=pltpu.CompilerParams(vmem_limit_bytes=vmem_bytes),
        name="pack",
    )(ids, section)


batch = 2


def inner_kernel(ids, section, order, low_radial, high_radial, acc, rows, lead, terms, fluxes):
    radial_pass(ids, section, low_radial, high_radial, rows, lead, terms, fluxes)
    theta_pass(section, order, acc, rows, lead, terms, fluxes)
    axial_inner(ids, section, acc, lead, terms)


def lead_faces(lead, terms, fluxes, columns):
    count = lead.shape[1] - 1

    def interface(r, carry):
        left = with_terms([lead[n, r, 0:columns] for n in range(5)])
        right = with_terms([lead[n, r + 1, 0:columns] for n in range(5)])
        for n, value in enumerate(interface_terms(left, right)):
            terms[n, r, 0:columns] = value
        return carry

    lax.fori_loop(0, count, interface, 0)

    def group_of(g, carry):
        p = g * batch

        def face(r, carry):
            flux = face_from(
                lambda n, s: terms[n, r + s, pl.ds(p, batch)],
                lambda n: lead[n, r + 2, pl.ds(p, batch)] + lead[n, r + 3, pl.ds(p, batch)],
            )
            for n, value in enumerate(flux):
                fluxes[n, r, pl.ds(p, batch)] = value
            return carry

        lax.fori_loop(0, count - 4, face, 0)
        return carry

    lax.fori_loop(0, columns // batch, group_of, 0)


def radial_pass(ids, section, low_radial, high_radial, rows, lead, terms, fluxes):
    planes, bands, width = section.shape[1:]
    tiles = width // lanes
    at_inner = ids[1] == 0
    at_outer = ids[1] == ids[2] - 1

    def spread(p, carry):
        for n, c in enumerate(radial_order):
            for j in range(tiles):
                rows[c, p, j * bands : (j + 1) * bands] = section[c, p, :, j * lanes : (j + 1) * lanes]
            for r in range(bands):
                lead[n, r + ghosts, p] = rows[c, p, pl.ds(r, tiles, stride=bands)]
            sign = -1.0 if c == 3 else 1.0
            for k in range(ghosts):
                wall_low = sign * rows[c, p, pl.ds(ghosts - 1 - k, tiles, stride=bands)]
                wall_high = sign * rows[c, p, pl.ds(bands - 1 - k, tiles, stride=bands)]
                lead[n, k, p] = jnp.where(at_inner, wall_low, low_radial[c, p, k])
                lead[n, bands + ghosts + k, p] = jnp.where(at_outer, wall_high, high_radial[c, p, k])
        return carry

    lax.fori_loop(0, planes, spread, 0)
    lead_faces(lead, terms, fluxes, planes)

    def gather(p, carry):
        for n, c in enumerate(radial_order):
            for r in range(bands):
                rows[c, p, pl.ds(r, tiles, stride=bands)] = fluxes[n, r + 1, p] - fluxes[n, r, p]
        return carry

    lax.fori_loop(0, planes, gather, 0)


def two_parts(values):
    high = values.astype(jnp.bfloat16)
    low = (values - high.astype(jnp.float32)).astype(jnp.bfloat16)
    return jnp.concatenate([high, low], axis=0)


def azimuthal_order(width):
    tiles = width // lanes
    cell = np.arange(width)
    matrix = np.zeros((width, width), np.float32)
    matrix[cell, cell % tiles * lanes + cell // tiles] = 1.0
    return jnp.asarray(matrix, jnp.bfloat16)


def theta_pass(section, order, acc, rows, lead, terms, fluxes):
    planes, bands, width = section.shape[1:]
    tiles = width // lanes
    half = 5 * planes * bands
    cells = jnp.concatenate([section[c].reshape(planes * bands, width) for c in theta_order], axis=0)
    both = jnp.dot(two_parts(cells), order[...], preferred_element_type=jnp.float32)
    both = (both[:half] + both[half:]).reshape(5, planes, bands, width)
    for n in range(5):
        for j in range(tiles):
            row = both[n, :, :, j * lanes : (j + 1) * lanes]
            lead[n, ghosts + j, 0:planes] = row
            if j < ghosts:
                lead[n, ghosts + tiles + j, 0:planes] = pltpu.roll(row, lanes - 1, 2)
            if j >= tiles - ghosts:
                lead[n, j + ghosts - tiles, 0:planes] = pltpu.roll(row, 1, 2)
    lead_faces(lead, terms, fluxes, planes)
    lane = lane_index((planes, bands, lanes))

    def flux(n, r):
        value = fluxes[n, r, 0:planes]
        if r < ghosts:
            return jnp.where(lane == 0, 0.0, value)
        if r > tiles - ghosts:
            return jnp.where(lane == lanes - 1, 0.0, value)
        return value

    changes = []
    for n in range(5):
        values = [flux(n, r) for r in range(tiles + 1)]
        parts = [values[r + 1] - values[r] for r in range(tiles)]
        changes.append(jnp.concatenate([v.reshape(planes * bands, lanes) for v in parts], axis=1))
    changes = two_parts(jnp.concatenate(changes, axis=0))
    both = lax.dot_general(changes, order[...], (((1,), (1,)), ((), ())), preferred_element_type=jnp.float32)
    both = (both[:half] + both[half:]).reshape(5, planes, bands, width)
    for n, c in enumerate(theta_order):
        for j in range(tiles):
            place = slice(j * lanes, (j + 1) * lanes)
            acc[c, 1 : planes + 1, :, place] = both[n, :, :, place] + rows[c, :, j * bands : (j + 1) * bands]


def axial_faces(count, first, acc, lead, terms):
    tiles = lead.shape[2]

    def interface(i, carry):
        left = with_terms([lead[n, i] for n in range(5)])
        right = with_terms([lead[n, i + 1] for n in range(5)])
        for n, value in enumerate(interface_terms(left, right)):
            terms[n, i] = value
        return carry

    lax.fori_loop(0, count + 4, interface, 0)

    def columns(g, carry):
        b0 = g * batch

        def face(i, carry):
            flux = face_from(
                lambda n, s: terms[n, i + s, pl.ds(b0, batch)],
                lambda n: lead[n, i + 2, pl.ds(b0, batch)] + lead[n, i + 3, pl.ds(b0, batch)],
            )
            for c, value in zip(axial_order, flux):
                for b in range(batch):
                    place = pl.ds(pl.multiple_of((b0 + b) * lanes, lanes), lanes)
                    acc[c, first + i, :, place] += value[b]
                    acc[c, first + i + 1, :, place] -= value[b]
            return carry

        lax.fori_loop(0, count, face, 0)
        return carry

    lax.fori_loop(0, tiles // batch, columns, 0)


def fill_plane(lead, section, at, plane):
    for c in axial_order:
        for j in range(section.shape[3] // lanes):
            lead[c, at, j] = section[c, plane, :, j * lanes : (j + 1) * lanes]


def axial_inner(ids, section, acc, lead, terms):
    planes, bands, width = section.shape[1:]
    first = jnp.where(ids[0] == 0, 0, ghosts)
    count = planes + 1 - ghosts
    for c in range(5):
        acc[c, 0] = jnp.zeros((bands, width), jnp.float32)
        acc[c, planes + 1] = jnp.zeros((bands, width), jnp.float32)

    def fill(i, carry):
        fill_plane(lead, section, i, jnp.clip(first + i - ghosts, 0, planes - 1))
        return carry

    lax.fori_loop(0, count + 5, fill, 0)
    axial_faces(count, first, acc, lead, terms)


def inner(ids, section, order, low_radial, high_radial):
    _, planes, bands, width = section.shape
    tiles = width // lanes
    depth = max(bands, tiles) + 2 * ghosts
    across = max(planes, tiles)
    vmem = pl.BlockSpec(memory_space=pltpu.VMEM)
    faces = (planes + 1) * tiles + planes * (tiles + bands + 2)
    return pl.pallas_call(
        inner_kernel,
        in_specs=[pl.BlockSpec(memory_space=pltpu.SMEM)] + [vmem] * 4,
        out_shape=jax.ShapeDtypeStruct((5, planes + 2, bands, width), jnp.float32),
        scratch_shapes=[
            pltpu.VMEM((5, planes, bands * tiles, lanes), jnp.float32),
            pltpu.VMEM((5, depth, across, 8, lanes), jnp.float32),
            pltpu.VMEM((16, depth - 1, across, 8, lanes), jnp.float32),
            pltpu.VMEM((5, depth - 5, planes, 8, lanes), jnp.float32),
        ],
        compiler_params=pltpu.CompilerParams(vmem_limit_bytes=vmem_bytes),
        cost_estimate=pl.CostEstimate(
            flops=faces * 8 * lanes * 700, bytes_accessed=section.size * 16, transcendentals=faces * 8 * lanes * 30
        ),
        name="inner",
    )(ids, section, order, low_radial, high_radial)


def mortar_planes(turn, near, far, window, write):
    _, _, bands, width = window.shape
    window[:, :, :, : near.shape[3]] = near[...]
    window[:, :, :, near.shape[3] :] = far[...]
    whole_tiles = turn[0] // lanes
    rest = turn[0] % lanes
    fraction = 0.25 * turn[1].astype(jnp.float32)
    source = lax.broadcasted_iota(jnp.int32, (2 * lanes, lanes), 0)
    target = lax.broadcasted_iota(jnp.int32, (2 * lanes, lanes), 1)
    gap = source + target - (lanes - 1 + rest)
    blend = jnp.where(gap == 0, 1.0 - fraction, jnp.where(gap == 1, fraction, 0.0)).astype(jnp.bfloat16)
    blend = jnp.concatenate([blend] * 3, axis=0)
    tiles = (width - chunk) // lanes
    for t in range(tiles):
        start = pl.multiple_of((tiles - 1 - t + whole_tiles) * lanes, lanes)
        cells = window[:, :, :, pl.ds(start, 2 * lanes)].reshape(5 * ghosts * bands, 2 * lanes)
        parts = []
        for _ in range(3):
            part = cells.astype(jnp.bfloat16)
            parts.append(part)
            cells = cells - part.astype(jnp.float32)
        mixed = jnp.dot(jnp.concatenate(parts, axis=1), blend, preferred_element_type=jnp.float32)
        mixed = mixed.reshape(5, ghosts, bands, lanes)
        for c in range(5):
            write(c, t, -mixed[c] if c == 2 else mixed[c])


def theta_edges(theta_own, left_high, right_low, acc):
    planes, bands, width = acc.shape[1] - 2, acc.shape[2], acc.shape[3]
    lane = lane_index((bands, lanes))
    at = lane % group
    inside = lane < group * planes
    cells = [
        jnp.where(inside & (at < ghosts), left_high[c], jnp.where(inside & (at >= group - ghosts), right_low[c], theta_own[c]))
        for c in theta_order
    ]
    turn = lambda value, shift: pltpu.roll(value, -shift % lanes, 1) if shift else value
    after = [turn(v, 1) for v in cells]
    terms = interface_terms(with_terms(cells), with_terms(after))
    flux = face_from(lambda n, s: turn(terms[n], s - 2), lambda n: cells[n] + after[n])
    low, high = ghosts - 1, group // 2 + 2
    wanted = inside & (((at >= low) & (at < low + 3)) | ((at >= high) & (at < high + 3)))
    for c, value in zip(theta_order, flux):
        value = jnp.where(wanted, value, 0.0)
        change = value - turn(value, -1)
        for p in range(planes):
            first = turn(change, group * p + ghosts)
            last = turn(change, group * p + high + ghosts - lanes)
            acc[c, p + 1, :, 0:lanes] += jnp.where(lane < ghosts, first, 0.0)
            acc[c, p + 1, :, width - lanes : width] += jnp.where(lane >= lanes - ghosts, last, 0.0)


def tail_kernel(ids, turn, section, base, acc, near, far, theta_own, left_high, right_low, out, lead, terms, window):
    planes, bands, width = section.shape[1:]
    front = ids[0] == 0
    kept = planes - 1
    own = jnp.where(front, 1, 0)
    own_at = jnp.where(front, 0, ghosts)
    ghost_at = jnp.where(front, kept, 0)
    first = jnp.where(front, planes + 1 - ghosts, 0)

    def fill(i, carry):
        fill_plane(lead, section, own_at + i, own + i)
        return carry

    lax.fori_loop(0, kept, fill, 0)

    def write(c, t, values):
        lead[c, pl.ds(ghost_at, ghosts), t] = values

    mortar_planes(turn, near, far, window, write)
    theta_edges(theta_own, left_high, right_low, acc)
    axial_faces(ghosts, first, acc, lead, terms)
    for c in range(5):

        def update(p, carry):
            change = (-0.25 * step_ratio / flux_scale) * acc[c, p + 1]
            out[c, p] = 0.75 * base[c, p] + (0.25 * section[c, p] + change)
            return carry

        lax.fori_loop(0, planes, update, 0)


def tail(ids, turn, section, base, acc, near, far, theta_own, left_high, right_low):
    _, planes, bands, width = section.shape
    tiles = width // lanes
    smem = pl.BlockSpec(memory_space=pltpu.SMEM)
    vmem = pl.BlockSpec(memory_space=pltpu.VMEM)
    anywhere = pl.BlockSpec(memory_space=pl.ANY)

    def kernel(ids, turn, section, base, acc_in, near, far, own, left, right, out, acc, lead, terms, window, sem):
        copy = pltpu.make_async_copy(acc_in, acc, sem)
        copy.start()
        copy.wait()
        tail_kernel(ids, turn, section, base, acc, near, far, own, left, right, out, lead, terms, window)

    return pl.pallas_call(
        kernel,
        in_specs=[smem, smem, vmem, vmem, anywhere] + [vmem] * 5,
        out_shape=jax.ShapeDtypeStruct(section.shape, jnp.float32),
        scratch_shapes=[
            pltpu.VMEM(acc.shape, jnp.float32),
            pltpu.VMEM((5, planes - 1 + ghosts, tiles, bands, lanes), jnp.float32),
            pltpu.VMEM((16, 2 * ghosts + 1, tiles, bands, lanes), jnp.float32),
            pltpu.VMEM((5, ghosts, bands, near.shape[3] + far.shape[3]), jnp.float32),
            pltpu.SemaphoreType.DMA(()),
        ],
        compiler_params=pltpu.CompilerParams(vmem_limit_bytes=vmem_bytes),
        name="tail",
    )(ids, turn, section, base, acc, near, far, theta_own, left_high, right_low)


def slab_routes(turns, slabs):
    both = []
    for ahead in (1, 0):
        both.append(
            [
                (block * slabs + slab, (1 - block) * slabs + (turns - ahead - slab) % slabs)
                for block in range(2)
                for slab in range(slabs)
            ]
        )
    return both


def exchange_and_step(ids, turn, order, base, section, near, far, transfer):
    slabs = lax.axis_size("theta")
    bands = lax.axis_size("radial")
    theta_low, theta_high, theta_own, radial_low, radial_high, near, far = pack(ids, section, near, far)
    near, far = transfer(near, far)
    low_radial = lax.ppermute(radial_high, "radial", [(i, i + 1) for i in range(bands - 1)])
    high_radial = lax.ppermute(radial_low, "radial", [(i + 1, i) for i in range(bands - 1)])
    left_high = lax.ppermute(theta_high, "theta", [(i, (i + 1) % slabs) for i in range(slabs)])
    right_low = lax.ppermute(theta_low, "theta", [((i + 1) % slabs, i) for i in range(slabs)])
    acc = inner(ids, section, order, low_radial, high_radial)
    return tail(ids, turn, section, base, acc, near, far, theta_own, left_high, right_low)


def shards(base_state, section_state, rotor_step):
    width = section_state.shape[3]
    slabs = lax.axis_size("theta")
    slab = lax.axis_index("theta")
    ids = jnp.stack([lax.axis_index("blk"), lax.axis_index("radial"), lax.axis_size("radial")]).astype(jnp.int32)
    step = rotor_step[0]
    offset = step // 4
    turns = offset // width
    start = offset % width
    cuts = width // chunk
    turn = jnp.stack([start % chunk, step % 4])
    order = azimuthal_order(width)

    if slabs > most_slabs:

        def gathered(near, far):
            facing = lax.ppermute(far, "blk", [(0, 1), (1, 0)])
            whole = lax.all_gather(facing, "theta", axis=3, tiled=True)
            doubled = jnp.concatenate([whole, whole, whole[..., :chunk]], axis=3)
            begin = (turns - 1 - slab) % slabs * width + start // chunk * chunk
            window = lax.dynamic_slice_in_dim(doubled, begin, width + chunk, 3)
            return window[..., :width], window[..., width:]

        return exchange_and_step(ids, turn, order, base_state, section_state, chunk, width, gathered)

    def branch(case):
        turned, cut = divmod(case, cuts)
        near_route, far_route = slab_routes(turned, slabs)

        def transfer(near, far):
            return (
                lax.ppermute(near, ("blk", "theta"), near_route),
                lax.ppermute(far, ("blk", "theta"), far_route),
            )

        def run(ids, turn, order, base, section):
            return exchange_and_step(
                ids, turn, order, base, section, width - cut * chunk, (cut + 1) * chunk, transfer
            )

        return run

    case = turns * cuts + start // chunk
    return lax.switch(case, [branch(i) for i in range(slabs * cuts)], ids, turn, order, base_state, section_state)


def solution(mesh):
    in_specs = (P(None, "blk", "radial", "theta"), P(None, "blk", "radial", "theta"), P())
    out_specs = P(None, "blk", "radial", "theta")
    return jax.shard_map(shards, mesh=mesh, in_specs=in_specs, out_specs=out_specs, check_vma=False)
```

profile of v0, /device:TPU:1, one launch (start us, length us, event | category | flops | bytes accessed | tf_op | source)
XLA Modules:
  0.0 51.3 jit_solution(918060006615763267)
XLA Ops:
  0.7 0.1 pad_add_fusion.1
  0.8 0.1 pad_add_fusion
  0.9 49.2 %conditional.1 = (f32[5,6,8,1024]{3,2,1,0:T(8,128)S(1)}) conditional(s32[]{:T(128)} %clamp.3, (s32[3]{0:T(128)S(1)}, f32[5,6,8,1024]{3,2,1,0:T(8,128)}, (), s32[2]{0:T(128)S(1)}, f32[5,6,8,1024]{3,2,1,0:T(8,128)}) %tuple.29, (s32[3]{0:T(128)S(1)}, f32[5,6,8,1024]{3,2,1,0:T(8,128)}, (), s32[2]{0:T(128)S(1)}, ...), branch_computations={%region_0.1_spmd, %region_1.2_spmd, %region_2.3_spmd, %region_3.4_... | conditional | flops 117555200 | bytes 26247500 | solution.py:575
  1.1 1.7 %pack.14 = (f32[5,8,128]{2,1,0:T(8,128)S(1)}, f32[5,8,128]{2,1,0:T(8,128)S(1)}, f32[5,8,128]{2,1,0:T(8,128)S(1)}, f32[5,6,3,8,128]{4,3,2,1,0:T(8,128)S(1)}, f32[...) custom-call(s32[3]{0:T(128)S(1)} %get-tuple-element.166.ids, ...), custom_call_target="tpu_custom_call" | custom-call | tf_op jit(solution)/shard_map/cond/branch_6_fun/pack/pallas_call | solution.py:179
  2.8 4.1 %collective-permute-start.38 = (f32[5,3,8,1024]{3,2,1,0:T(8,128)S(1)}, f32[5,3,8,1024]{3,2,1,0:T(8,128)S(1)}, u32[]{:S(2)}, u32[]{:S(2)}) collective-permute-start(f32[5,3,8,1024]{3,2,1,0:T(8,128)S(1)} %get-tuple-element.173), channel_id=1, source_target_pairs={{0,24},{4,20},{8,16},{12,28},{16,8},{20,4},{24,0},{28,12},{1,25},{... | collective-permute-start | bytes 1474568 | tf_op jit(solution)/shard_map/cond/branch_6_fun/ppermute | solution.py:563
  7.0 4.0 %collective-permute-start.36 = (f32[5,6,3,8,128]{4,3,2,1,0:T(8,128)S(1)}, f32[5,6,3,8,128]{4,3,2,1,0:T(8,128)S(1)}, u32[]{:S(2)}, u32[]{:S(2)}) collective-permute-start(f32[5,6,3,8,128]{4,3,2,1,0:T(8,128)S(1)} %get-tuple-element.171), channel_id=1, source_target_pairs={{0,1},{1,2},{2,3},{4,5},{5,6},{6,7},{8,9},{9,10},{10,11},{12,13},{... | collective-permute-start | bytes 1105928 | tf_op jit(solution)/shard_map/cond/branch_6_fun/ppermute | solution.py:524
  11.0 1.9 %collective-permute-start.37 = (f32[5,6,3,8,128]{4,3,2,1,0:T(8,128)S(1)}, f32[5,6,3,8,128]{4,3,2,1,0:T(8,128)S(1)}, u32[]{:S(2)}, u32[]{:S(2)}) collective-permute-start(f32[5,6,3,8,128]{4,3,2,1,0:T(8,128)S(1)} %get-tuple-element.172), channel_id=1, source_target_pairs={{1,0},{2,1},{3,2},{5,4},{6,5},{7,6},{9,8},{10,9},{11,10},{13,12},{... | collective-permute-start | bytes 1105928 | tf_op jit(solution)/shard_map/cond/branch_6_fun/ppermute | solution.py:525
  12.9 1.3 %collective-permute-start.39 = (f32[5,3,8,512]{3,2,1,0:T(8,128)S(1)}, f32[5,3,8,512]{3,2,1,0:T(8,128)S(1)}, u32[]{:S(2)}, u32[]{:S(2)}) collective-permute-start(f32[5,3,8,512]{3,2,1,0:T(8,128)S(1)} %get-tuple-element.174), channel_id=1, source_target_pairs={{0,28},{4,24},{8,20},{12,16},{16,12},{20,8},{24,4},{28,0},{1,29},{... | collective-permute-start | bytes 737288 | tf_op jit(solution)/shard_map/cond/branch_6_fun/ppermute | solution.py:564
  14.2 0.0 collective-permute-start.40
  14.2 1.2 %collective-permute-done.36.low_radial = f32[5,6,3,8,128]{4,3,2,1,0:T(8,128)S(1)} collective-permute-done((f32[5,6,3,8,128]{4,3,2,1,0:T(8,128)S(1)}, f32[5,6,3,8,128]{4,3,2,1,0:T(8,128)S(1)}, u32[]{:S(2)}, u32[]{:S(2)}) %collective-permute-start.36) | collective-permute-done | bytes 368672 | tf_op jit(solution)/shard_map/cond/branch_6_fun/ppermute | solution.py:524
  15.4 2.1 %collective-permute-start.41 = (f32[5,8,128]{2,1,0:T(8,128)S(1)}, f32[5,8,128]{2,1,0:T(8,128)S(1)}, u32[]{:S(2)}, u32[]{:S(2)}) collective-permute-start(f32[5,8,128]{2,1,0:T(8,128)S(1)} %get-tuple-element.177), channel_id=1, source_target_pairs={{4,0},{8,4},{12,8},{0,12},{5,1},{9,5},{13,9},{1,13},{6,2},{10,6},{... | collective-permute-start | bytes 61448 | tf_op jit(solution)/shard_map/cond/branch_6_fun/ppermute | solution.py:527
  17.5 2.6 %collective-permute-done.37.high_radial = f32[5,6,3,8,128]{4,3,2,1,0:T(8,128)S(1)} collective-permute-done((f32[5,6,3,8,128]{4,3,2,1,0:T(8,128)S(1)}, f32[5,6,3,8,128]{4,3,2,1,0:T(8,128)S(1)}, u32[]{:S(2)}, u32[]{:S(2)}) %collective-permute-start.37) | collective-permute-done | bytes 368672 | tf_op jit(solution)/shard_map/cond/branch_6_fun/ppermute | solution.py:525
  20.1 0.0 copy-start.5
  20.1 1.6 %copy-done.5 = bf16[1024,1024]{1,0:T(8,128)(2,1)S(1)} copy-done((bf16[1024,1024]{1,0:T(8,128)(2,1)S(1)}, bf16[1024,1024]{1,0:T(8,128)(2,1)}, u32[]{:S(2)}) %copy-start.5) | copy-done | bytes 2097176 | tf_op jit(solution)/shard_map/cond
  21.7 0.0 copy-start.14
  21.7 0.0 copy-start.22
  21.7 21.9 %inner.14.acc_in = f32[5,8,8,1024]{3,2,1,0:T(8,128)S(1)} custom-call(s32[3]{0:T(128)S(1)} %get-tuple-element.166.ids, f32[5,6,8,1024]{3,2,1,0:T(8,128)} %get-tuple-element.221.section, bf16[1024,1024]{1,0:T(8,128)(2,1)S(1)} %copy-done.5, f32[5,6,3,8,128]{4,3,2,1,0:T(8,128)S(1)} %collective-permute-done.36.low_radial, ...), custom_call_target="tpu_custom_call" | custom-call | flops 117555200 | bytes 3932160 | tf_op jit(solution)/shard_map/cond/branch_6_fun/inner/pallas_call | solution.py:376
  43.6 0.0 collective-permute-done.40.left
  43.6 0.0 collective-permute-done.41.right
  43.6 0.0 collective-permute-done.39.far
  43.6 0.0 collective-permute-done.38.near
  43.6 0.0 copy-done.14
  43.6 0.0 copy-done.22
  43.6 5.0 %tail.14 = f32[5,6,8,1024]{3,2,1,0:T(8,128)S(1)} custom-call(s32[3]{0:T(128)S(1)} %get-tuple-element.166.ids, s32[2]{0:T(128)S(1)} %get-tuple-element.167.turn, f32[5,6,8,1024]{3,2,1,0:T(8,128)S(1)} %copy-done.14, f32[5,6,8,1024]{3,2,1,0:T(8,128)S(1)} %copy-done.22, f32[5,8,8,1024]{3,2,1,0:T(8,128)S(1)} %inner.14.acc_in, ...), custom_call_target="tpu_custom_call" | custom-call | tf_op jit(solution)/shard_map/cond/branch_6_fun/tail/pallas_call | solution.py:490
  50.1 0.0 copy-start.24
  50.1 0.9 %copy-done.24 = f32[5,6,8,1024]{3,2,1,0:T(8,128)} copy-done((f32[5,6,8,1024]{3,2,1,0:T(8,128)}, f32[5,6,8,1024]{3,2,1,0:T(8,128)S(1)}, u32[]{:S(2)}) %copy-start.24) | copy-done | bytes 983064
Async XLA Ops:
  2.8 40.8 %collective-permute-start.38 = (f32[5,3,8,1024]{3,2,1,0:T(8,128)S(1)}, f32[5,3,8,1024]{3,2,1,0:T(8,128)S(1)}, u32[]{:S(2)}, u32[]{:S(2)}) collective-permute-start(f32[5,3,8,1024]{3,2,1,0:T(8,128)S(1)} %get-tuple-element.173), channel_id=1, source_target_pairs={{0,24},{4,20},{8,16},{12,28},{16,8},{20,4},{24,0},{28,12},{1,25},{... | collective-permute-start | bytes 1474568 | tf_op jit(solution)/shard_map/cond/branch_6_fun/ppermute | solution.py:563
  7.0 8.4 %collective-permute-start.36 = (f32[5,6,3,8,128]{4,3,2,1,0:T(8,128)S(1)}, f32[5,6,3,8,128]{4,3,2,1,0:T(8,128)S(1)}, u32[]{:S(2)}, u32[]{:S(2)}) collective-permute-start(f32[5,6,3,8,128]{4,3,2,1,0:T(8,128)S(1)} %get-tuple-element.171), channel_id=1, source_target_pairs={{0,1},{1,2},{2,3},{4,5},{5,6},{6,7},{8,9},{9,10},{10,11},{12,13},{... | collective-permute-start | bytes 1105928 | tf_op jit(solution)/shard_map/cond/branch_6_fun/ppermute | solution.py:524
  11.0 9.1 %collective-permute-start.37 = (f32[5,6,3,8,128]{4,3,2,1,0:T(8,128)S(1)}, f32[5,6,3,8,128]{4,3,2,1,0:T(8,128)S(1)}, u32[]{:S(2)}, u32[]{:S(2)}) collective-permute-start(f32[5,6,3,8,128]{4,3,2,1,0:T(8,128)S(1)} %get-tuple-element.172), channel_id=1, source_target_pairs={{1,0},{2,1},{3,2},{5,4},{6,5},{7,6},{9,8},{10,9},{11,10},{13,12},{... | collective-permute-start | bytes 1105928 | tf_op jit(solution)/shard_map/cond/branch_6_fun/ppermute | solution.py:525
  12.9 30.7 %collective-permute-start.39 = (f32[5,3,8,512]{3,2,1,0:T(8,128)S(1)}, f32[5,3,8,512]{3,2,1,0:T(8,128)S(1)}, u32[]{:S(2)}, u32[]{:S(2)}) collective-permute-start(f32[5,3,8,512]{3,2,1,0:T(8,128)S(1)} %get-tuple-element.174), channel_id=1, source_target_pairs={{0,28},{4,24},{8,20},{12,16},{16,12},{20,8},{24,4},{28,0},{1,29},{... | collective-permute-start | bytes 737288 | tf_op jit(solution)/shard_map/cond/branch_6_fun/ppermute | solution.py:564
  14.2 29.4 %collective-permute-start.40 = (f32[5,8,128]{2,1,0:T(8,128)S(1)}, f32[5,8,128]{2,1,0:T(8,128)S(1)}, u32[]{:S(2)}, u32[]{:S(2)}) collective-permute-start(f32[5,8,128]{2,1,0:T(8,128)S(1)} %get-tuple-element.176), channel_id=1, source_target_pairs={{0,4},{4,8},{8,12},{12,0},{1,5},{5,9},{9,13},{13,1},{2,6},{6,10},{... | collective-permute-start | bytes 61448 | tf_op jit(solution)/shard_map/cond/branch_6_fun/ppermute | solution.py:526
  15.4 28.2 %collective-permute-start.41 = (f32[5,8,128]{2,1,0:T(8,128)S(1)}, f32[5,8,128]{2,1,0:T(8,128)S(1)}, u32[]{:S(2)}, u32[]{:S(2)}) collective-permute-start(f32[5,8,128]{2,1,0:T(8,128)S(1)} %get-tuple-element.177), channel_id=1, source_target_pairs={{4,0},{8,4},{12,8},{0,12},{5,1},{9,5},{13,9},{1,13},{6,2},{10,6},{... | collective-permute-start | bytes 61448 | tf_op jit(solution)/shard_map/cond/branch_6_fun/ppermute | solution.py:527
  20.1 1.6 %copy-start.5 = (bf16[1024,1024]{1,0:T(8,128)(2,1)S(1)}, bf16[1024,1024]{1,0:T(8,128)(2,1)}, u32[]{:S(2)}) copy-start(bf16[1024,1024]{1,0:T(8,128)(2,1)} %constant.82.clone.7.order) | copy-start | bytes 6291460 | tf_op jit(solution)/shard_map/cond
  21.7 22.0 %copy-start.14 = (f32[5,6,8,1024]{3,2,1,0:T(8,128)S(1)}, f32[5,6,8,1024]{3,2,1,0:T(8,128)}, u32[]{:S(2)}) copy-start(f32[5,6,8,1024]{3,2,1,0:T(8,128)} %get-tuple-element.221.section) | copy-start | bytes 2949124 | tf_op jit(solution)/shard_map/cond
  21.7 22.0 %copy-start.22 = (f32[5,6,8,1024]{3,2,1,0:T(8,128)S(1)}, f32[5,6,8,1024]{3,2,1,0:T(8,128)}, u32[]{:S(2)}) copy-start(f32[5,6,8,1024]{3,2,1,0:T(8,128)} %get-tuple-element.237.base) | copy-start | bytes 2949124 | tf_op jit(solution)/shard_map/cond
  50.1 0.9 %copy-start.24 = (f32[5,6,8,1024]{3,2,1,0:T(8,128)}, f32[5,6,8,1024]{3,2,1,0:T(8,128)S(1)}, u32[]{:S(2)}) copy-start(f32[5,6,8,1024]{3,2,1,0:T(8,128)S(1)} %get-tuple-element.343) | copy-start | bytes 2949124
where the time goes:
time: 50.6 us; the launch traced here: 51.3 us
  Pallas kernels  28.7 us (57%)
  starting transfers between devices  13.5 us (27%)
  waiting for transfers between devices  3.78 us (7%)
  local copies, waits for them, and re-layouts  2.54 us (5%)
  loops' own time  1.73 us (3%)
  between operations  0.98 us (2%)
    pallas_call x1, Pallas kernels, inner(): pl.pallas_call(inner_kernel, in_specs=[pl.BlockSpec(memory_space=pltpu.SM...  21.9 us
    pallas_call x1, Pallas kernels, tail(): pl.pallas_call(kernel, in_specs=[smem, smem, vmem, vmem, anywhere] + [vme...  5.02 us
    ppermute x1, starting transfers between devices, transfer(): lax.ppermute(near, ('blk', 'theta'), near_route)  4.13 us
    ppermute x1, starting transfers between devices, exchange_and_step(): lax.ppermute(radial_high, 'radial', [(i, i + 1) for i in range(bands - 1)])  3.98 us
    ppermute x1, waiting for transfers between devices, exchange_and_step(): lax.ppermute(radial_low, 'radial', [(i + 1, i) for i in range(bands - 1)])  2.6 us
    ppermute x1, starting transfers between devices, exchange_and_step(): lax.ppermute(theta_low, 'theta', [((i + 1) % slabs, i) for i in range(sla...  2.09 us
    ppermute x1, starting transfers between devices, exchange_and_step(): lax.ppermute(radial_low, 'radial', [(i + 1, i) for i in range(bands - 1)])  1.92 us
    pallas_call x1, Pallas kernels, pack(): pl.pallas_call(pack_kernel, in_specs=[pl.BlockSpec(memory_space=pltpu.SME...  1.75 us
  transfers between devices with their start and end apart: 6, of which 2 were waited for; matrix products, arithmetic and copies ran while one was open for 0% of the time, Pallas kernels for 43%

commit v1 on v0

v1 whole, which is shorter than its diff:
```python
import functools

import jax
import jax.numpy as jnp
from jax import lax
from jax.experimental import pallas as pl
from jax.experimental.pallas import tpu as pltpu
from jax.sharding import PartitionSpec as P

gamma_ratio = 1.4
weno_epsilon = 1e-06
step_ratio = 0.12
lanes = 128
ghosts = 3
group = 16
batch = 2
flux_scale = 12.0
most_slabs = 8
vmem_bytes = 48 * 1024 * 1024

axial_order = (0, 1, 2, 3, 4)
radial_order = (0, 3, 1, 2, 4)
theta_order = (0, 2, 1, 3, 4)


def inverse(value):
    guess = pl.reciprocal(value, approx=True)
    return guess * (2.0 - value * guess)


def cell_terms(state):
    density, normal, first, second, energy = state
    inv = inverse(density)
    speed = normal * inv
    kinetic = 0.5 * (normal * normal + first * first + second * second) * inv
    pressure = (gamma_ratio - 1.0) * (energy - kinetic)
    square = gamma_ratio * pressure * inv
    wave = jnp.abs(speed) + square * lax.rsqrt(square)
    flux = (normal, normal * speed + pressure, first * speed, second * speed, (energy + pressure) * speed)
    return flux, wave


def interface_terms(left, right):
    (state_l, flux_l, wave_l), (state_r, flux_r, wave_r) = left, right
    return (
        [r - l for l, r in zip(state_l, state_r)]
        + [r - l for l, r in zip(flux_l, flux_r)]
        + [0.5 * flux_scale * (r + l) for l, r in zip(flux_l, flux_r)]
        + [jnp.maximum(wave_l, wave_r)]
    )


def weno_terms(d0, d1, d2, d3, epsilon):
    e0 = d1 - d0
    e1 = d2 - d1
    e2 = d3 - d2
    f0 = e0 - e1
    f1 = e1 - e2
    t1 = 0.75 * d1
    t2 = 0.75 * d2
    shared = t1 * d2 + epsilon
    low = e0 * e0 + (t1 * f0 + shared)
    mid = e1 * e1 + shared
    high = e2 * e2 + (t2 * f1 + shared)
    x = mid * pl.reciprocal(low, approx=True)
    y = mid * pl.reciprocal(high, approx=True)
    weight_low = x * x
    weight_high = 1.5 * (y * y)
    total = 0.5 * weight_low + (weight_high + 3.0)
    return (weight_low * f0 + weight_high * f1) * pl.reciprocal(total, approx=True)


def face_terms(diff_state, diff_flux, sum_state, sum_flux, wave):
    inv = inverse(sum_state(0))
    un, va, vb, specific = (inv * sum_state(k) for k in range(1, 5))
    half = 0.5 * (un * un + va * va + vb * vb)
    internal = specific - half
    square = gamma_ratio * (gamma_ratio - 1.0) * internal
    inv_sound = lax.rsqrt(square)
    sound = square * inv_sound
    factor = (gamma_ratio - 1.0) * inv_sound * inv_sound
    enthalpy = specific + (gamma_ratio - 1.0) * internal

    def project(dens, norm, first, second, energy):
        sn = norm - un * dens
        sa = first - va * dens
        sb = second - vb * dens
        even = factor * (energy - half * dens - un * sn - va * sa - vb * sb)
        odd = inv_sound * sn
        return even - odd, dens - even, sa, sb, even + odd

    def side(vectors):
        chars = [project(*vector) for vector in vectors]
        return [weno_terms(*(c[k] for c in chars), weno_epsilon * (12.0 if k in (0, 4) else 3.0)) for k in range(5)]

    plus = [[diff_flux[s](c) + wave * diff_state[s](c) for c in range(5)] for s in range(4)]
    forward = side(plus)
    minus = [[diff_flux[s](c) - wave * diff_state[s](c) for c in range(5)] for s in range(4, 0, -1)]
    backward = side(minus)
    central = [sum_flux(c) + (plus[1][c] - plus[2][c]) + (minus[2][c] - minus[1][c]) for c in range(5)]
    wave_minus, entropy, sa, sb, wave_plus = (f - b for f, b in zip(forward, backward))
    even = 0.5 * (wave_plus + wave_minus)
    odd = sound * (0.5 * (wave_plus - wave_minus))
    carried = even + entropy
    return (
        central[0] + carried,
        central[1] + un * carried + odd,
        central[2] + va * carried + sa,
        central[3] + vb * carried + sb,
        central[4] + enthalpy * even + un * odd + half * entropy + va * sa + vb * sb,
    )


def face_from(load, sum_state):
    return face_terms(
        [functools.partial(lambda s, c: load(c, s), s) for s in range(5)],
        [functools.partial(lambda s, c: load(5 + c, s), s) for s in range(5)],
        sum_state,
        lambda c: load(10 + c, 2),
        load(15, 2),
    )


def with_terms(state):
    return (state, *cell_terms(state))


def lane_index(shape):
    return lax.broadcasted_iota(jnp.int32, shape, len(shape) - 1)


def tile_rows(state):
    components, planes, bands, width = state.shape
    split = state.reshape(components, planes, bands, width // lanes, lanes)
    return split.transpose(0, 1, 3, 2, 4).reshape(components, planes, -1, lanes)


def from_tile_rows(rows, bands):
    components, planes, count, _ = rows.shape
    split = rows.reshape(components, planes, count // bands, bands, lanes)
    return split.transpose(0, 1, 3, 2, 4).reshape(components, planes, bands, -1)


def loop(count, body):
    def step(i, carry):
        body(i)
        return carry

    lax.fori_loop(0, count, step, 0)


def make_order(order):
    width = order.shape[0]
    tiles = width // lanes

    def order_rows(t):
        row = lax.broadcasted_iota(jnp.int32, (lanes, width), 0) + t * lanes
        column = lax.broadcasted_iota(jnp.int32, (lanes, width), 1)
        target = row % tiles * lanes + row // tiles
        order[pl.ds(pl.multiple_of(t * lanes, lanes), lanes)] = jnp.where(column == target, 1.0, 0.0).astype(jnp.bfloat16)

    loop(tiles, order_rows)


def store_split(split, n, tile, values):
    high = values.astype(jnp.bfloat16)
    low = (values - high.astype(jnp.float32)).astype(jnp.bfloat16)
    flat = values.shape[0]
    start = pl.multiple_of(n * flat, 16)
    split[pl.ds(start, flat), tile * lanes : (tile + 1) * lanes] = high
    split[pl.ds(5 * flat + start, flat), tile * lanes : (tile + 1) * lanes] = low


def reorder(section, cells, split, order):
    _, tiles, planes, bands, _ = cells.shape
    flat = planes * bands
    for n, c in enumerate(theta_order):
        for t in range(tiles):
            store_split(split, n, t, section[c, :, t * bands : (t + 1) * bands].reshape(flat, lanes))
    both = jnp.dot(split[...], order[...], preferred_element_type=jnp.float32)
    both = both[: 5 * flat] + both[5 * flat :]
    for n in range(5):
        for j in range(tiles):
            part = both[n * flat : (n + 1) * flat, j * lanes : (j + 1) * lanes]
            cells[n, j] = part.reshape(planes, bands, lanes)


def restore(split, order, planes, acc):
    tiles = order.shape[0] // lanes
    flat = split.shape[0] // 10
    bands = flat // planes
    both = lax.dot_general(split[...], order[...], (((1,), (1,)), ((), ())), preferred_element_type=jnp.float32)
    both = both[: 5 * flat] + both[5 * flat :]
    for n, c in enumerate(theta_order):
        for t in range(tiles):
            part = both[n * flat : (n + 1) * flat, t * lanes : (t + 1) * lanes]
            acc[c, 1 : planes + 1, t * bands : (t + 1) * bands] = part.reshape(planes, bands, lanes)


def pack_kernel(
    bands, ids, turn, section,
    held, theta_low, theta_high, theta_own, radial_low, radial_high, whole, part, cells, order, split
):
    planes, rows = section.shape[1:3]
    tiles = rows // bands
    facing = jnp.where(ids[0] == 0, planes - ghosts, 0)
    part_at = pl.multiple_of(turn[2] * part.shape[2], bands)
    lane = lane_index((bands, lanes))

    def component(c):
        held[c] = section[c]
        for i in range(ghosts):
            whole[c, i] = section[c, facing + i]
            part[c, i] = section[c, facing + i, pl.ds(part_at, part.shape[2])]
        own = jnp.full((bands, lanes), (1.0, 0.0, 0.0, 0.0, 3.0)[c], jnp.float32)
        low = high = own
        for p in range(planes):
            at = lane - group * p
            first = section[c, p, 0:bands]
            last = section[c, p, rows - bands : rows]
            own_first = pltpu.roll(first, group * p + ghosts, 1)
            own_last = pltpu.roll(last, group * p + group - ghosts, 1)
            sent_low = pltpu.roll(first, group * p + group - ghosts, 1)
            sent_high = pltpu.roll(last, group * p + ghosts, 1)
            own = jnp.where((at >= ghosts) & (at < group // 2), own_first, own)
            own = jnp.where((at >= group // 2) & (at < group - ghosts), own_last, own)
            low = jnp.where((at >= group - ghosts) & (at < group), sent_low, low)
            high = jnp.where((at >= 0) & (at < ghosts), sent_high, high)
        theta_own[c] = own
        theta_low[c] = low
        theta_high[c] = high

        for p in range(planes):
            for k in range(ghosts):
                radial_low[c, p, k] = section[c, p, pl.ds(k, tiles, stride=bands)]
                radial_high[c, p, k] = section[c, p, pl.ds(bands - ghosts + k, tiles, stride=bands)]

    for c in range(5):
        component(c)
    make_order(order)
    reorder(section, cells, split, order)


def pack(ids, turn, section, bands):
    _, planes, rows, _ = section.shape
    smem = pl.BlockSpec(memory_space=pltpu.SMEM)
    vmem = pl.BlockSpec(memory_space=pltpu.VMEM)
    array = lambda *shape: jax.ShapeDtypeStruct(shape, jnp.float32)
    theta = array(5, bands, lanes)
    radial = array(5, planes, ghosts, rows // bands, lanes)
    mortar = [array(5, ghosts, rows, lanes), array(5, ghosts, rows // 2, lanes)]
    width = rows // bands * lanes
    cells = array(5, rows // bands, planes, bands, lanes)
    order = jax.ShapeDtypeStruct((width, width), jnp.bfloat16)
    return pl.pallas_call(
        functools.partial(pack_kernel, bands),
        in_specs=[smem, smem, vmem],
        out_specs=[vmem] * 10,
        out_shape=(array(*section.shape), theta, theta, theta, radial, radial, *mortar, cells, order),
        scratch_shapes=[pltpu.VMEM((10 * planes * bands, width), jnp.bfloat16)],
        compiler_params=pltpu.CompilerParams(vmem_limit_bytes=vmem_bytes),
        name="pack",
    )(ids, turn, section)


def inner_kernel(bands, ids, section, cells, low_radial, high_radial, acc, split, lead, terms, fluxes):
    radial_pass(bands, ids, section, low_radial, high_radial, acc, lead, terms, fluxes)
    theta_pass(cells, lead, terms, fluxes, split)
    axial_inner(ids, section, acc, lead, terms)


def lead_faces(lead, cells, columns, terms, emit):
    def column_group(g):
        p = g * batch

        def state(r):
            return [lead[n, r, pl.ds(p, batch)] for n in range(5)]

        def cell(r):
            here = state(r)
            flux, wave = cell_terms(here)
            return here, flux, wave

        def keep(r, values):
            for n, value in enumerate((*values[1], values[2])):
                terms[16 + n, r] = value

        def interface(r, right):
            left = (state(r), [terms[16 + n, r] for n in range(5)], terms[21, r])
            for n, value in enumerate(interface_terms(left, right)):
                terms[n, r] = value

        left = cell(0)
        for r in range(5):
            right = cell(r + 1)
            for n, value in enumerate(interface_terms(left, right)):
                terms[n, r] = value
            left = right
        keep(5, left)

        def face(r):
            flux = face_from(
                lambda n, s: terms[n, r + s],
                lambda n: lead[n, r + 2, pl.ds(p, batch)] + lead[n, r + 3, pl.ds(p, batch)],
            )
            emit(r, p, flux)
            right = cell(jnp.minimum(r + 6, cells - 1))
            interface(r + 5, right)
            keep(r + 6, right)

        loop(cells - 5, face)

    loop(columns // batch, column_group)


def keep_flux(fluxes, r, p, flux):
    for n, value in enumerate(flux):
        fluxes[n, r, pl.ds(p, batch)] = value


def radial_pass(bands, ids, section, low_radial, high_radial, acc, lead, terms, fluxes):
    planes, rows = section.shape[1:3]
    tiles = rows // bands
    at_inner = ids[1] == 0
    at_outer = ids[1] == ids[2] - 1

    def spread(p):
        for n, c in enumerate(radial_order):
            band = [section[c, p, pl.ds(r, tiles, stride=bands)] for r in range(bands)]
            sign = -1.0 if c == 3 else 1.0
            for r in range(bands):
                lead[n, r + ghosts, p] = band[r]
            for k in range(ghosts):
                lead[n, k, p] = jnp.where(at_inner, sign * band[ghosts - 1 - k], low_radial[c, p, k])
                lead[n, bands + ghosts + k, p] = jnp.where(at_outer, sign * band[bands - 1 - k], high_radial[c, p, k])

    loop(planes, spread)
    lead_faces(lead, bands + 2 * ghosts, planes, terms, functools.partial(keep_flux, fluxes))

    def gather(p):
        for n, c in enumerate(radial_order):
            for r in range(bands):
                acc[c, p + 1, pl.ds(r, tiles, stride=bands)] = fluxes[n, r + 1, p] - fluxes[n, r, p]

    loop(planes, gather)


def theta_pass(cells, lead, terms, fluxes, split):
    _, tiles, planes, bands, _ = cells.shape

    def fill(n):
        for j in range(tiles):
            lead[n, ghosts + j, 0:planes] = cells[n, j]
        for k in range(ghosts):
            lead[n, k, 0:planes] = pltpu.roll(cells[n, tiles - ghosts + k], 1, 2)
            lead[n, ghosts + tiles + k, 0:planes] = pltpu.roll(cells[n, k], lanes - 1, 2)

    loop(5, fill)
    lead_faces(lead, tiles + 2 * ghosts, planes, terms, functools.partial(keep_flux, fluxes))
    lane = lane_index((planes, bands, lanes))

    def changes(n):
        before = None
        for r in range(tiles + 1):
            flux = fluxes[n, r, 0:planes]
            if r < ghosts:
                flux = jnp.where(lane == 0, 0.0, flux)
            if r > tiles - ghosts:
                flux = jnp.where(lane == lanes - 1, 0.0, flux)
            if r > 0:
                store_split(split, n, r - 1, (flux - before).reshape(planes * bands, lanes))
            before = flux

    loop(5, changes)


def axial_faces(count, first, acc, lead, terms):
    tiles, bands = lead.shape[2:4]

    def emit(i, p, flux):
        place = pl.ds(pl.multiple_of(p * bands, bands), batch * bands)
        for c, value in zip(axial_order, flux):
            value = value.reshape(batch * bands, lanes)
            acc[c, first + i, place] += value
            acc[c, first + i + 1, place] -= value

    lead_faces(lead, count + 5, tiles, terms, emit)


def axial_inner(ids, section, acc, lead, terms):
    planes = section.shape[1]
    tiles, bands = lead.shape[2:4]
    first = jnp.where(ids[0] == 0, 0, ghosts)
    count = planes + 1 - ghosts
    for c in range(5):
        acc[c, 0] = jnp.zeros(acc.shape[2:], jnp.float32)
        acc[c, planes + 1] = jnp.zeros(acc.shape[2:], jnp.float32)

    def fill(i):
        plane = jnp.clip(first + i - ghosts, 0, planes - 1)
        for c in axial_order:
            lead[c, i] = section[c, plane].reshape(tiles, bands, lanes)

    loop(count + 5, fill)
    axial_faces(count, first, acc, lead, terms)


def inner(ids, section, cells, bands, low_radial, high_radial):
    _, planes, rows, _ = section.shape
    tiles = rows // bands
    depth = max(bands, tiles) + 2 * ghosts
    across = max(planes, tiles)
    vmem = pl.BlockSpec(memory_space=pltpu.VMEM)
    faces = (planes + 1) * tiles + planes * (tiles + bands + 2)
    return pl.pallas_call(
        functools.partial(inner_kernel, bands),
        in_specs=[pl.BlockSpec(memory_space=pltpu.SMEM)] + [vmem] * 4,
        out_shape=(
            jax.ShapeDtypeStruct((5, planes + 2, rows, lanes), jnp.float32),
            jax.ShapeDtypeStruct((10 * planes * bands, tiles * lanes), jnp.bfloat16),
        ),
        scratch_shapes=[
            pltpu.VMEM((5, depth, across, 8, lanes), jnp.float32),
            pltpu.VMEM((22, depth + 1, batch, 8, lanes), jnp.float32),
            pltpu.VMEM((5, depth - 5, planes, 8, lanes), jnp.float32),
        ],
        compiler_params=pltpu.CompilerParams(vmem_limit_bytes=vmem_bytes),
        cost_estimate=pl.CostEstimate(
            flops=faces * 8 * lanes * 700, bytes_accessed=section.size * 16, transcendentals=faces * 8 * lanes * 30
        ),
        name="inner",
    )(ids, section, cells, low_radial, high_radial)


def mortar_planes(turn, whole, part, window, lead, at):
    tiles, bands = lead.shape[2:4]
    whole_at = pl.multiple_of(jnp.where(turn[2] == 0, 0, part.shape[2]), bands)
    part_at = pl.multiple_of(jnp.where(turn[2] == 0, whole.shape[2], 0), bands)
    for c in range(5):
        window[c, :, pl.ds(whole_at, whole.shape[2])] = whole[c]
        window[c, :, pl.ds(part_at, part.shape[2])] = part[c]
    skipped = turn[0] // lanes
    rest = turn[0] % lanes
    fraction = 0.25 * turn[1].astype(jnp.float32)
    source = lax.broadcasted_iota(jnp.int32, (2 * lanes, lanes), 0)
    target = lax.broadcasted_iota(jnp.int32, (2 * lanes, lanes), 1)
    gap = source + target - (lanes - 1 + rest)
    blend = jnp.where(gap == 0, 1.0 - fraction, jnp.where(gap == 1, fraction, 0.0)).astype(jnp.bfloat16)
    blend = jnp.concatenate([blend[:lanes]] * 3 + [blend[lanes:]] * 3, axis=0)

    def parts_of(tile):
        start = pl.multiple_of((tile + skipped) * bands, bands)
        cells = window[:, :, pl.ds(start, bands)].reshape(5 * ghosts * bands, lanes)
        parts = []
        for _ in range(3):
            parts.append(cells.astype(jnp.bfloat16))
            cells = cells - parts[-1].astype(jnp.float32)
        return parts

    after = parts_of(tiles)
    for t in range(tiles):
        here = parts_of(tiles - 1 - t)
        mixed = jnp.dot(jnp.concatenate(here + after, axis=1), blend, preferred_element_type=jnp.float32)
        mixed = mixed.reshape(5, ghosts, bands, lanes)
        for c in range(5):
            lead[c, pl.ds(at, ghosts), t] = -mixed[c] if c == 2 else mixed[c]
        after = here


def theta_edges(theta_own, left_high, right_low, acc):
    planes, rows = acc.shape[1] - 2, acc.shape[2]
    bands = theta_own.shape[1]
    lane = lane_index((bands, lanes))
    at = lane % group
    inside = lane < group * planes
    cells = [
        jnp.where(inside & (at < ghosts), left_high[c], jnp.where(inside & (at >= group - ghosts), right_low[c], theta_own[c]))
        for c in theta_order
    ]
    turn = lambda value, shift: pltpu.roll(value, -shift % lanes, 1) if shift else value
    after = [turn(v, 1) for v in cells]
    terms = interface_terms(with_terms(cells), with_terms(after))
    flux = face_from(lambda n, s: turn(terms[n], s - 2), lambda n: cells[n] + after[n])
    low, high = ghosts - 1, group // 2 + 2
    wanted = inside & (((at >= low) & (at < low + 3)) | ((at >= high) & (at < high + 3)))
    flux = [jnp.where(wanted, value, 0.0) for value in flux]
    changes = [value - turn(value, -1) for value in flux]

    for p in range(planes):
        for c, change in zip(theta_order, changes):
            first = turn(change, group * p + ghosts)
            last = turn(change, group * p + high + ghosts - lanes)
            acc[c, p + 1, 0:bands] += jnp.where(lane < ghosts, first, 0.0)
            acc[c, p + 1, rows - bands : rows] += jnp.where(lane >= lanes - ghosts, last, 0.0)


def tail_kernel(
    ids, turn, section, base_state, acc, split, order, whole, part, theta_own, left_high, right_low, out_state,
    more, lead, terms, window, base, out, sems
):
    loading = pltpu.make_async_copy(base_state, base, sems.at[0])
    loading.start()
    planes = section.shape[1]
    tiles, bands = lead.shape[2:4]
    front = ids[0] == 0
    kept = planes - 1
    own = jnp.where(front, 1, 0)
    own_at = jnp.where(front, 0, ghosts)
    ghost_at = jnp.where(front, kept, 0)
    first = jnp.where(front, planes + 1 - ghosts, 0)

    def fill(i):
        for c in axial_order:
            lead[c, own_at + i] = section[c, own + i].reshape(tiles, bands, lanes)

    loop(kept, fill)

    for c in range(5):
        more[c, 0] = jnp.zeros(more.shape[2:], jnp.float32)
        more[c, planes + 1] = jnp.zeros(more.shape[2:], jnp.float32)
    restore(split, order, planes, more)
    mortar_planes(turn, whole, part, window, lead, ghost_at)
    theta_edges(theta_own, left_high, right_low, more)
    axial_faces(ghosts, first, more, lead, terms)

    loading.wait()
    storing = [pltpu.make_async_copy(out.at[c], out_state.at[c], sems.at[c]) for c in range(5)]
    for c in range(5):
        change = (-0.25 * step_ratio / flux_scale) * (acc[c, 1 : planes + 1] + more[c, 1 : planes + 1])
        out[c] = 0.75 * base[c] + (0.25 * section[c] + change)
        storing[c].start()
    for copy in storing:
        copy.wait()


def tail(ids, turn, section, base, acc, split, order, whole, part, theta_own, left_high, right_low):
    _, planes, rows, _ = section.shape
    bands = theta_own.shape[1]
    tiles = rows // bands
    smem = pl.BlockSpec(memory_space=pltpu.SMEM)
    vmem = pl.BlockSpec(memory_space=pltpu.VMEM)
    anywhere = pl.BlockSpec(memory_space=pl.ANY)
    return pl.pallas_call(
        tail_kernel,
        in_specs=[smem, smem, vmem, anywhere] + [vmem] * 8,
        out_specs=anywhere,
        out_shape=jax.ShapeDtypeStruct(section.shape, jnp.float32),
        scratch_shapes=[
            pltpu.VMEM(acc.shape, jnp.float32),
            pltpu.VMEM((5, planes - 1 + ghosts, tiles, bands, lanes), jnp.float32),
            pltpu.VMEM((22, 2 * ghosts + 3, batch, bands, lanes), jnp.float32),
            pltpu.VMEM((5, ghosts, whole.shape[2] + part.shape[2], lanes), jnp.float32),
            pltpu.VMEM(section.shape, jnp.float32),
            pltpu.VMEM(section.shape, jnp.float32),
            pltpu.SemaphoreType.DMA((5,)),
        ],
        compiler_params=pltpu.CompilerParams(vmem_limit_bytes=vmem_bytes),
        name="tail",
    )(ids, turn, section, base, acc, split, order, whole, part, theta_own, left_high, right_low)


def slab_routes(turns, slabs):
    both = []
    for ahead in (1, 0):
        both.append(
            [
                (block * slabs + slab, (1 - block) * slabs + (turns - ahead - slab) % slabs)
                for block in range(2)
                for slab in range(slabs)
            ]
        )
    return both


def shards(base_state, section_state, rotor_step):
    bands, width = section_state.shape[2:]
    rows = width // lanes * bands
    slabs = lax.axis_size("theta")
    slab = lax.axis_index("theta")
    parts = lax.axis_size("radial")
    ids = jnp.stack([lax.axis_index("blk"), lax.axis_index("radial"), parts]).astype(jnp.int32)
    step = rotor_step[0]
    offset = step // 4
    turns = offset // width
    start = offset % width
    second_half = start // (width // 2)
    turn = jnp.stack([start % (width // 2), step % 4, second_half])
    base, section = tile_rows(base_state), tile_rows(section_state)
    section, theta_low, theta_high, theta_own, radial_low, radial_high, whole, part, cells, order = pack(
        ids, turn, section, bands
    )

    def halos(radial_low, radial_high, theta_low, theta_high):
        return (
            lax.ppermute(radial_high, "radial", [(i, i + 1) for i in range(parts - 1)]),
            lax.ppermute(radial_low, "radial", [(i + 1, i) for i in range(parts - 1)]),
            lax.ppermute(theta_high, "theta", [(i, (i + 1) % slabs) for i in range(slabs)]),
            lax.ppermute(theta_low, "theta", [((i + 1) % slabs, i) for i in range(slabs)]),
        )

    if slabs > most_slabs:
        low_radial, high_radial, left_high, right_low = halos(radial_low, radial_high, theta_low, theta_high)
        facing = lax.ppermute(whole, "blk", [(0, 1), (1, 0)])
        ring = lax.all_gather(facing, "theta", axis=2, tiled=True)
        ring = jnp.concatenate([ring, ring, ring[:, :, : rows // 2]], axis=2)
        begin = (turns - 1 - slab) % slabs * rows + second_half * (rows // 2)
        whole = lax.dynamic_slice_in_dim(ring, begin, rows, 2)
        part = lax.dynamic_slice_in_dim(ring, begin + rows, rows // 2, 2)
        turn = turn.at[2].set(0)
        acc, split = inner(ids, section, cells, bands, low_radial, high_radial)
    else:

        def branch(case):
            near, far = slab_routes(case // 2 + 1, slabs)
            whole_route, part_route = (near, far) if case % 2 == 0 else (far, near)

            def run(ids, section, cells, whole, part, *ends):
                whole = lax.ppermute(whole, ("blk", "theta"), whole_route)
                part = lax.ppermute(part, ("blk", "theta"), part_route)
                low_radial, high_radial, left_high, right_low = halos(*ends)
                acc, split = inner(ids, section, cells, bands, low_radial, high_radial)
                return acc, split, whole, part, left_high, right_low

            return run

        case = (turns - 1) * 2 + second_half
        branches = [branch(i) for i in range((slabs - 1) * 2)]
        ends = (radial_low, radial_high, theta_low, theta_high)
        acc, split, whole, part, left_high, right_low = lax.switch(
            case, branches, ids, section, cells, whole, part, *ends
        )
    out = tail(ids, turn, section, base, acc, split, order, whole, part, theta_own, left_high, right_low)
    return from_tile_rows(out, bands)


def solution(mesh):
    in_specs = (P(None, "blk", "radial", "theta"), P(None, "blk", "radial", "theta"), P())
    out_specs = P(None, "blk", "radial", "theta")
    return jax.shard_map(shards, mesh=mesh, in_specs=in_specs, out_specs=out_specs, check_vma=False)
```

time: 50.6 us -> 48.3 us (0.955); the launches traced: 51.3 us -> 48 us
  loops' own time: 1.73 us -> 0.07 us
  local copies, waits for them, and re-layouts: 2.54 us -> 1.21 us
  waiting for transfers between devices: 3.78 us -> 4.51 us
  starting transfers between devices: 13.5 us -> 12.8 us
    another operation x1, loops' own time: 1.73 us -> 0.07 us  [shards(): lax.switch(case, branches, ids, section, cells, whole, part, *ends)]
    cond x6 -> x0, local copies, waits for them, and re-layouts: 1.6 us -> none
    ppermute x6, waiting for transfers between devices: 3.78 us -> 4.51 us  [the longest x1 3.5 us: halos(): lax.ppermute(radial_low, 'radial', [(i + 1, i) for i in range(parts - 1)])]
    ppermute x6, starting transfers between devices: 13.5 us -> 12.8 us  [the longest x1 4.07 us: run(): whole = lax.ppermute(whole, ('blk', 'theta'), whole_route)]
    unnamed x2 -> x4, local copies, waits for them, and re-layouts: 0.94 us -> 1.21 us
  transfers between devices with their start and end apart: 6 -> 6, of which waited for: 2 -> 2; matrix products, arithmetic and copies ran while one was open for 0% -> 0% of each run, Pallas kernels for 43% -> 37%
where the time goes in v1:
time: 48.3 us; the launch traced here: 48 us
  Pallas kernels  28.6 us (59%)
  starting transfers between devices  12.8 us (27%)
  waiting for transfers between devices  4.51 us (9%)
  local copies, waits for them, and re-layouts  1.21 us (3%)
  between operations  0.76 us (2%)
    pallas_call x1, Pallas kernels, inner(): pl.pallas_call(functools.partial(inner_kernel, bands), in_specs=[pl.Block...  17.8 us
    pallas_call x1, Pallas kernels, tail(): pl.pallas_call(tail_kernel, in_specs=[smem, smem, vmem, anywhere] + [vmem...  7.28 us
    ppermute x1, starting transfers between devices, run(): whole = lax.ppermute(whole, ('blk', 'theta'), whole_route)  4.07 us
    ppermute x1, starting transfers between devices, halos(): lax.ppermute(radial_high, 'radial', [(i, i + 1) for i in range(parts - 1)])  3.98 us
    pallas_call x1, Pallas kernels, pack(): pl.pallas_call(functools.partial(pack_kernel, bands), in_specs=[smem, sme...  3.58 us
    ppermute x1, waiting for transfers between devices, halos(): lax.ppermute(radial_low, 'radial', [(i + 1, i) for i in range(parts - 1)])  3.5 us
    ppermute x1, starting transfers between devices, halos(): lax.ppermute(radial_low, 'radial', [(i + 1, i) for i in range(parts - 1)])  1.92 us
    ppermute x1, starting transfers between devices, halos(): lax.ppermute(theta_high, 'theta', [(i, (i + 1) % slabs) for i in range(sl...  1.42 us
  transfers between devices with their start and end apart: 6, of which 2 were waited for; matrix products, arithmetic and copies ran while one was open for 0% of the time, Pallas kernels for 37%

profile of v1, /device:TPU:1, one launch (start us, length us, event | category | flops | bytes accessed | tf_op | source)
XLA Modules:
  0.0 48.0 jit_solution(2879850439831508303)
XLA Ops:
  0.7 0.1 pad_add_fusion
  0.8 0.0 copy-start
  0.8 1.2 %copy-done = f32[5,6,8,1024]{3,2,1,0:T(8,128)S(1)} copy-done((f32[5,6,8,1024]{3,2,1,0:T(8,128)S(1)}, f32[5,6,8,1024]{3,2,1,0:T(8,128)}, u32[]{:S(2)}) %copy-start) | copy-done | bytes 983064
  2.0 3.6 %pack.1 = (f32[5,6,64,128]{3,2,1,0:T(8,128)}, f32[5,8,128]{2,1,0:T(8,128)S(1)}, f32[5,8,128]{2,1,0:T(8,128)S(1)}, f32[5,8,128]{2,1,0:T(8,128)S(1)}, f32[5,6,3,8,...) custom-call(s32[3]{0:T(128)S(1)} %get-tuple-element.211.ids, ...), custom_call_target="tpu_custom_call" | custom-call | tf_op jit(solution)/shard_map/pack/pallas_call | solution.py:255
  5.6 0.0 copy-start.1
  5.6 35.1 %conditional.1 = (f32[5,8,64,128]{3,2,1,0:T(8,128)S(1)}, bf16[480,1024]{1,0:T(8,128)(2,1)S(1)}, f32[5,3,64,128]{3,2,1,0:T(8,128)}, f32[5,3,32,128]{3,2,1,0:T(8,1...) conditional(s32[]{:T(128)} %clamp.3, (f32[5,6,3,8,128]{4,3,2,1,0:T(8,128)S(1)}, ...), branch_computations={%region_0.1_spmd, %region_1.2_spmd, %region_2.3_spmd, %region_3.4_... | conditional | flops 117555200 | bytes 9994528 | solution.py:629
  5.6 4.1 %collective-permute-start.20 = (f32[5,3,64,128]{3,2,1,0:T(8,128)S(1)}, f32[5,3,64,128]{3,2,1,0:T(8,128)}, u32[]{:S(2)}, u32[]{:S(2)}) collective-permute-start(f32[5,3,64,128]{3,2,1,0:T(8,128)S(1)} %get-tuple-element.153), channel_id=1, source_target_pairs={{0,24},{4,20},{8,16},{12,28},{16,8},{20,4},{24,0},{28,12},{1,25},{... | collective-permute-start | bytes 1474568 | tf_op jit(solution)/shard_map/cond/branch_3_fun/ppermute | solution.py:618
  9.7 4.0 %collective-permute-start.18 = (f32[5,6,3,8,128]{4,3,2,1,0:T(8,128)S(1)}, f32[5,6,3,8,128]{4,3,2,1,0:T(8,128)S(1)}, u32[]{:S(2)}, u32[]{:S(2)}) collective-permute-start(f32[5,6,3,8,128]{4,3,2,1,0:T(8,128)S(1)} %get-tuple-element.149), channel_id=1, source_target_pairs={{0,1},{1,2},{2,3},{4,5},{5,6},{6,7},{8,9},{9,10},{10,11},{12,13},{... | collective-permute-start | bytes 1105928 | tf_op jit(solution)/shard_map/cond/branch_3_fun/ppermute | solution.py:595
  13.7 1.9 %collective-permute-start.19 = (f32[5,6,3,8,128]{4,3,2,1,0:T(8,128)S(1)}, f32[5,6,3,8,128]{4,3,2,1,0:T(8,128)S(1)}, u32[]{:S(2)}, u32[]{:S(2)}) collective-permute-start(f32[5,6,3,8,128]{4,3,2,1,0:T(8,128)S(1)} %get-tuple-element.150), channel_id=1, source_target_pairs={{1,0},{2,1},{3,2},{5,4},{6,5},{7,6},{9,8},{10,9},{11,10},{13,12},{... | collective-permute-start | bytes 1105928 | tf_op jit(solution)/shard_map/cond/branch_3_fun/ppermute | solution.py:596
  15.6 0.1 collective-permute-start.21
  15.7 1.4 %collective-permute-start.22 = (f32[5,8,128]{2,1,0:T(8,128)S(1)}, f32[5,8,128]{2,1,0:T(8,128)}, u32[]{:S(2)}, u32[]{:S(2)}) collective-permute-start(f32[5,8,128]{2,1,0:T(8,128)S(1)} %get-tuple-element.155), channel_id=1, source_target_pairs={{0,4},{4,8},{8,12},{12,0},{1,5},{5,9},{9,13},{13,1},{2,6},{6,10},{... | collective-permute-start | bytes 61448 | tf_op jit(solution)/shard_map/cond/branch_3_fun/ppermute | solution.py:597
  17.1 1.0 %collective-permute-done.18.low_radial = f32[5,6,3,8,128]{4,3,2,1,0:T(8,128)S(1)} collective-permute-done((f32[5,6,3,8,128]{4,3,2,1,0:T(8,128)S(1)}, f32[5,6,3,8,128]{4,3,2,1,0:T(8,128)S(1)}, u32[]{:S(2)}, u32[]{:S(2)}) %collective-permute-start.18) | collective-permute-done | bytes 368672 | tf_op jit(solution)/shard_map/cond/branch_3_fun/ppermute | solution.py:595
  18.1 1.3 %collective-permute-start.23 = (f32[5,8,128]{2,1,0:T(8,128)S(1)}, f32[5,8,128]{2,1,0:T(8,128)}, u32[]{:S(2)}, u32[]{:S(2)}) collective-permute-start(f32[5,8,128]{2,1,0:T(8,128)S(1)} %get-tuple-element.156), channel_id=1, source_target_pairs={{4,0},{8,4},{12,8},{0,12},{5,1},{9,5},{13,9},{1,13},{6,2},{10,6},{... | collective-permute-start | bytes 61448 | tf_op jit(solution)/shard_map/cond/branch_3_fun/ppermute | solution.py:598
  19.4 3.5 %collective-permute-done.19.high_radial = f32[5,6,3,8,128]{4,3,2,1,0:T(8,128)S(1)} collective-permute-done((f32[5,6,3,8,128]{4,3,2,1,0:T(8,128)S(1)}, f32[5,6,3,8,128]{4,3,2,1,0:T(8,128)S(1)}, u32[]{:S(2)}, u32[]{:S(2)}) %collective-permute-start.19) | collective-permute-done | bytes 368672 | tf_op jit(solution)/shard_map/cond/branch_3_fun/ppermute | solution.py:596
  22.9 17.8 %inner.9 = (f32[5,8,64,128]{3,2,1,0:T(8,128)S(1)}, bf16[480,1024]{1,0:T(8,128)(2,1)S(1)}) custom-call(s32[3]{0:T(128)S(1)} %get-tuple-element.146.ids, f32[5,6,64,128]{3,2,1,0:T(8,128)} %get-tuple-element.147.section, f32[5,8,6,8,128]{4,3,2,1,0:T(8,128)S(1)} %get-tuple-element.148.cells, f32[5,6,3,8,128]{4,3,2,1,0:T(8,128)S(1)} %collective-permute-done.18.low_radial, ...), custom_call_target="tpu_custom_call" | custom-call | flops 117555200 | bytes 3932160 | tf_op jit(solution)/shard_map/cond/branch_3_fun/inner/pallas_call | solution.py:415
  40.7 0.0 collective-permute-done.22
  40.7 0.0 collective-permute-done.23
  40.7 0.0 collective-permute-done.21
  40.7 0.0 collective-permute-done.20
  40.7 0.0 copy-done.1
  40.7 7.3 %tail.1 = f32[5,6,64,128]{3,2,1,0:T(8,128)} custom-call(s32[3]{0:T(128)S(1)} %get-tuple-element.211.ids, s32[3]{0:T(128)S(1)} %get-tuple-element.212.turn, f32[5,6,64,128]{3,2,1,0:T(8,128)} %get-tuple-element.195.section, f32[5,6,64,128]{3,2,1,0:T(8,128)S(1)} %bitcast.26, f32[5,8,64,128]{3,2,1,0:T(8,128)S(1)} %get-tuple-element.203.acc, ...), custom_call_target="tpu_custom_call" | custom-call | tf_op jit(solution)/shard_map/tail/pallas_call | solution.py:543
Async XLA Ops:
  0.8 1.2 %copy-start = (f32[5,6,8,1024]{3,2,1,0:T(8,128)S(1)}, f32[5,6,8,1024]{3,2,1,0:T(8,128)}, u32[]{:S(2)}) copy-start(f32[5,6,8,1024]{3,2,1,0:T(8,128)} %param.10) | copy-start | bytes 2949124
  5.6 35.1 %copy-start.1 = (f32[5,6,8,1024]{3,2,1,0:T(8,128)S(1)}, f32[5,6,8,1024]{3,2,1,0:T(8,128)}, u32[]{:S(2)}) copy-start(f32[5,6,8,1024]{3,2,1,0:T(8,128)} %param.9) | copy-start | bytes 2949124
  5.6 35.1 %collective-permute-start.20 = (f32[5,3,64,128]{3,2,1,0:T(8,128)S(1)}, f32[5,3,64,128]{3,2,1,0:T(8,128)}, u32[]{:S(2)}, u32[]{:S(2)}) collective-permute-start(f32[5,3,64,128]{3,2,1,0:T(8,128)S(1)} %get-tuple-element.153), channel_id=1, source_target_pairs={{0,24},{4,20},{8,16},{12,28},{16,8},{20,4},{24,0},{28,12},{1,25},{... | collective-permute-start | bytes 1474568 | tf_op jit(solution)/shard_map/cond/branch_3_fun/ppermute | solution.py:618
  9.7 8.4 %collective-permute-start.18 = (f32[5,6,3,8,128]{4,3,2,1,0:T(8,128)S(1)}, f32[5,6,3,8,128]{4,3,2,1,0:T(8,128)S(1)}, u32[]{:S(2)}, u32[]{:S(2)}) collective-permute-start(f32[5,6,3,8,128]{4,3,2,1,0:T(8,128)S(1)} %get-tuple-element.149), channel_id=1, source_target_pairs={{0,1},{1,2},{2,3},{4,5},{5,6},{6,7},{8,9},{9,10},{10,11},{12,13},{... | collective-permute-start | bytes 1105928 | tf_op jit(solution)/shard_map/cond/branch_3_fun/ppermute | solution.py:595
  13.7 9.2 %collective-permute-start.19 = (f32[5,6,3,8,128]{4,3,2,1,0:T(8,128)S(1)}, f32[5,6,3,8,128]{4,3,2,1,0:T(8,128)S(1)}, u32[]{:S(2)}, u32[]{:S(2)}) collective-permute-start(f32[5,6,3,8,128]{4,3,2,1,0:T(8,128)S(1)} %get-tuple-element.150), channel_id=1, source_target_pairs={{1,0},{2,1},{3,2},{5,4},{6,5},{7,6},{9,8},{10,9},{11,10},{13,12},{... | collective-permute-start | bytes 1105928 | tf_op jit(solution)/shard_map/cond/branch_3_fun/ppermute | solution.py:596
  15.6 25.1 %collective-permute-start.21 = (f32[5,3,32,128]{3,2,1,0:T(8,128)S(1)}, f32[5,3,32,128]{3,2,1,0:T(8,128)}, u32[]{:S(2)}, u32[]{:S(2)}) collective-permute-start(f32[5,3,32,128]{3,2,1,0:T(8,128)S(1)} %get-tuple-element.154), channel_id=1, source_target_pairs={{0,20},{4,16},{8,28},{12,24},{16,4},{20,0},{24,12},{28,8},{1,21},{... | collective-permute-start | bytes 737288 | tf_op jit(solution)/shard_map/cond/branch_3_fun/ppermute | solution.py:619
  15.7 25.0 %collective-permute-start.22 = (f32[5,8,128]{2,1,0:T(8,128)S(1)}, f32[5,8,128]{2,1,0:T(8,128)}, u32[]{:S(2)}, u32[]{:S(2)}) collective-permute-start(f32[5,8,128]{2,1,0:T(8,128)S(1)} %get-tuple-element.155), channel_id=1, source_target_pairs={{0,4},{4,8},{8,12},{12,0},{1,5},{5,9},{9,13},{13,1},{2,6},{6,10},{... | collective-permute-start | bytes 61448 | tf_op jit(solution)/shard_map/cond/branch_3_fun/ppermute | solution.py:597
  18.1 22.6 %collective-permute-start.23 = (f32[5,8,128]{2,1,0:T(8,128)S(1)}, f32[5,8,128]{2,1,0:T(8,128)}, u32[]{:S(2)}, u32[]{:S(2)}) collective-permute-start(f32[5,8,128]{2,1,0:T(8,128)S(1)} %get-tuple-element.156), channel_id=1, source_target_pairs={{4,0},{8,4},{12,8},{0,12},{5,1},{9,5},{13,9},{1,13},{6,2},{10,6},{... | collective-permute-start | bytes 61448 | tf_op jit(solution)/shard_map/cond/branch_3_fun/ppermute | solution.py:598

commit v2 on v1

--- a/solution.py
+++ b/solution.py
@@ -15,8 +15,9 @@
 group = 16
 batch = 2
 flux_scale = 12.0
+flux_factor = -0.25 * step_ratio / flux_scale
 most_slabs = 8
-vmem_bytes = 48 * 1024 * 1024
+vmem_bytes = 32 * 1024 * 1024
 
 axial_order = (0, 1, 2, 3, 4)
 radial_order = (0, 3, 1, 2, 4)
@@ -93,9 +94,11 @@
         chars = [project(*vector) for vector in vectors]
         return [weno_terms(*(c[k] for c in chars), weno_epsilon * (12.0 if k in (0, 4) else 3.0)) for k in range(5)]
 
-    plus = [[diff_flux[s](c) + wave * diff_state[s](c) for c in range(5)] for s in range(4)]
+    fluxes = [[diff_flux[s](c) for c in range(5)] for s in range(5)]
+    damped = [[wave * diff_state[s](c) for c in range(5)] for s in range(5)]
+    plus = [[f + d for f, d in zip(fluxes[s], damped[s])] for s in range(4)]
     forward = side(plus)
-    minus = [[diff_flux[s](c) - wave * diff_state[s](c) for c in range(5)] for s in range(4, 0, -1)]
+    minus = [[f - d for f, d in zip(fluxes[s], damped[s])] for s in range(4, 0, -1)]
     backward = side(minus)
     central = [sum_flux(c) + (plus[1][c] - plus[2][c]) + (minus[2][c] - minus[1][c]) for c in range(5)]
     wave_minus, entropy, sa, sb, wave_plus = (f - b for f, b in zip(forward, backward))
@@ -150,16 +153,15 @@
 
 
 def make_order(order):
-    width = order.shape[0]
-    tiles = width // lanes
-
-    def order_rows(t):
-        row = lax.broadcasted_iota(jnp.int32, (lanes, width), 0) + t * lanes
-        column = lax.broadcasted_iota(jnp.int32, (lanes, width), 1)
-        target = row % tiles * lanes + row // tiles
-        order[pl.ds(pl.multiple_of(t * lanes, lanes), lanes)] = jnp.where(column == target, 1.0, 0.0).astype(jnp.bfloat16)
-
-    loop(tiles, order_rows)
+    tiles = order.shape[0] // lanes
+    row = lax.broadcasted_iota(jnp.int32, (lanes, lanes), 0)
+    column = lax.broadcasted_iota(jnp.int32, (lanes, lanes), 1)
+    for t in range(tiles):
+        meets = column - row // tiles == t * lanes // tiles
+        key = jnp.where(meets, row % tiles, -1).astype(jnp.float32).astype(jnp.bfloat16)
+        for j in range(tiles):
+            block = jnp.where(key == j, 1.0, 0.0).astype(jnp.bfloat16)
+            order[t * lanes : (t + 1) * lanes, j * lanes : (j + 1) * lanes] = block
 
 
 def store_split(split, n, tile, values):
@@ -199,12 +201,14 @@
 
 def pack_kernel(
     bands, ids, turn, section,
-    held, theta_low, theta_high, theta_own, radial_low, radial_high, whole, part, cells, order, split
+    held, even_theta, odd_theta, theta_own, even_radial, odd_radial, whole, part, cells, order, split
 ):
     planes, rows = section.shape[1:3]
     tiles = rows // bands
     facing = jnp.where(ids[0] == 0, planes - ghosts, 0)
     part_at = pl.multiple_of(turn[2] * part.shape[2], bands)
+    even = ids[1] % 2 == 0
+    even_slab = ids[3] % 2 == 0
     lane = lane_index((bands, lanes))
 
     def component(c):
@@ -227,13 +231,15 @@
             low = jnp.where((at >= group - ghosts) & (at < group), sent_low, low)
             high = jnp.where((at >= 0) & (at < ghosts), sent_high, high)
         theta_own[c] = own
-        theta_low[c] = low
-        theta_high[c] = high
+        even_theta[c] = jnp.where(even_slab, high, low)
+        odd_theta[c] = jnp.where(even_slab, low, high)
 
         for p in range(planes):
             for k in range(ghosts):
-                radial_low[c, p, k] = section[c, p, pl.ds(k, tiles, stride=bands)]
-                radial_high[c, p, k] = section[c, p, pl.ds(bands - ghosts + k, tiles, stride=bands)]
+                low = section[c, p, pl.ds(k, tiles, stride=bands)]
+                high = section[c, p, pl.ds(bands - ghosts + k, tiles, stride=bands)]
+                even_radial[c, p, k] = jnp.where(even, high, low)
+                odd_radial[c, p, k] = jnp.where(even, low, high)
 
     for c in range(5):
         component(c)
@@ -263,10 +269,19 @@
     )(ids, turn, section)
 
 
-def inner_kernel(bands, ids, section, cells, low_radial, high_radial, acc, split, lead, terms, fluxes):
-    radial_pass(bands, ids, section, low_radial, high_radial, acc, lead, terms, fluxes)
+def inner_kernel(
+    bands, ids, section, cells, even_radial, odd_radial, base_state, acc, split, lead, terms, fluxes, base, sem
+):
+    planes = section.shape[1]
+    loading = pltpu.make_async_copy(base_state, base, sem)
+    loading.start()
+    radial_pass(bands, ids, section, even_radial, odd_radial, acc, lead, terms, fluxes)
     theta_pass(cells, lead, terms, fluxes, split)
     axial_inner(ids, section, acc, lead, terms)
+    loading.wait()
+    for c in range(5):
+        change = flux_factor * acc[c, 1 : planes + 1]
+        acc[c, 1 : planes + 1] = 0.75 * base[c] + (0.25 * section[c] + change)
 
 
 def lead_faces(lead, cells, columns, terms, emit):
@@ -318,11 +333,12 @@
         fluxes[n, r, pl.ds(p, batch)] = value
 
 
-def radial_pass(bands, ids, section, low_radial, high_radial, acc, lead, terms, fluxes):
+def radial_pass(bands, ids, section, even_radial, odd_radial, acc, lead, terms, fluxes):
     planes, rows = section.shape[1:3]
     tiles = rows // bands
     at_inner = ids[1] == 0
     at_outer = ids[1] == ids[2] - 1
+    even = ids[1] % 2 == 0
 
     def spread(p):
         for n, c in enumerate(radial_order):
@@ -331,8 +347,10 @@
             for r in range(bands):
                 lead[n, r + ghosts, p] = band[r]
             for k in range(ghosts):
-                lead[n, k, p] = jnp.where(at_inner, sign * band[ghosts - 1 - k], low_radial[c, p, k])
-                lead[n, bands + ghosts + k, p] = jnp.where(at_outer, sign * band[bands - 1 - k], high_radial[c, p, k])
+                one, two = even_radial[c, p, k], odd_radial[c, p, k]
+                low, high = jnp.where(even, two, one), jnp.where(even, one, two)
+                lead[n, k, p] = jnp.where(at_inner, sign * band[ghosts - 1 - k], low)
+                lead[n, bands + ghosts + k, p] = jnp.where(at_outer, sign * band[bands - 1 - k], high)
 
     loop(planes, spread)
     lead_faces(lead, bands + 2 * ghosts, planes, terms, functools.partial(keep_flux, fluxes))
@@ -405,7 +423,7 @@
     axial_faces(count, first, acc, lead, terms)
 
 
-def inner(ids, section, cells, bands, low_radial, high_radial):
+def inner(ids, section, cells, bands, even_radial, odd_radial, base):
     _, planes, rows, _ = section.shape
     tiles = rows // bands
     depth = max(bands, tiles) + 2 * ghosts
@@ -414,7 +432,7 @@
     faces = (planes + 1) * tiles + planes * (tiles + bands + 2)
     return pl.pallas_call(
         functools.partial(inner_kernel, bands),
-        in_specs=[pl.BlockSpec(memory_space=pltpu.SMEM)] + [vmem] * 4,
+        in_specs=[pl.BlockSpec(memory_space=pltpu.SMEM)] + [vmem] * 4 + [pl.BlockSpec(memory_space=pl.ANY)],
         out_shape=(
             jax.ShapeDtypeStruct((5, planes + 2, rows, lanes), jnp.float32),
             jax.ShapeDtypeStruct((10 * planes * bands, tiles * lanes), jnp.bfloat16),
@@ -423,22 +441,19 @@
             pltpu.VMEM((5, depth, across, 8, lanes), jnp.float32),
             pltpu.VMEM((22, depth + 1, batch, 8, lanes), jnp.float32),
             pltpu.VMEM((5, depth - 5, planes, 8, lanes), jnp.float32),
+            pltpu.VMEM(section.shape, jnp.float32),
+            pltpu.SemaphoreType.DMA(()),
         ],
         compiler_params=pltpu.CompilerParams(vmem_limit_bytes=vmem_bytes),
         cost_estimate=pl.CostEstimate(
             flops=faces * 8 * lanes * 700, bytes_accessed=section.size * 16, transcendentals=faces * 8 * lanes * 30
         ),
         name="inner",
-    )(ids, section, cells, low_radial, high_radial)
-
-
-def mortar_planes(turn, whole, part, window, lead, at):
+    )(ids, section, cells, even_radial, odd_radial, base)
+
+
+def mortar_planes(turn, window, lead, at):
     tiles, bands = lead.shape[2:4]
-    whole_at = pl.multiple_of(jnp.where(turn[2] == 0, 0, part.shape[2]), bands)
-    part_at = pl.multiple_of(jnp.where(turn[2] == 0, whole.shape[2], 0), bands)
-    for c in range(5):
-        window[c, :, pl.ds(whole_at, whole.shape[2])] = whole[c]
-        window[c, :, pl.ds(part_at, part.shape[2])] = part[c]
     skipped = turn[0] // lanes
     rest = turn[0] % lanes
     fraction = 0.25 * turn[1].astype(jnp.float32)
@@ -467,16 +482,18 @@
         after = here
 
 
-def theta_edges(theta_own, left_high, right_low, acc):
+def theta_edges(even, theta_own, even_theta, odd_theta, acc):
     planes, rows = acc.shape[1] - 2, acc.shape[2]
     bands = theta_own.shape[1]
     lane = lane_index((bands, lanes))
     at = lane % group
     inside = lane < group * planes
-    cells = [
-        jnp.where(inside & (at < ghosts), left_high[c], jnp.where(inside & (at >= group - ghosts), right_low[c], theta_own[c]))
-        for c in theta_order
-    ]
+    cells = []
+    for c in theta_order:
+        left = jnp.where(even, odd_theta[c], even_theta[c])
+        right = jnp.where(even, even_theta[c], odd_theta[c])
+        own = jnp.where(inside & (at >= group - ghosts), right, theta_own[c])
+        cells.append(jnp.where(inside & (at < ghosts), left, own))
     turn = lambda value, shift: pltpu.roll(value, -shift % lanes, 1) if shift else value
     after = [turn(v, 1) for v in cells]
     terms = interface_terms(with_terms(cells), with_terms(after))
@@ -495,13 +512,19 @@
 
 
 def tail_kernel(
-    ids, turn, section, base_state, acc, split, order, whole, part, theta_own, left_high, right_low, out_state,
-    more, lead, terms, window, base, out, sems
+    ids, turn, section, acc, split, order, whole, part, theta_own, even_theta, odd_theta, out_state,
+    more, lead, terms, window, out, sems
 ):
-    loading = pltpu.make_async_copy(base_state, base, sems.at[0])
-    loading.start()
     planes = section.shape[1]
     tiles, bands = lead.shape[2:4]
+    whole_at = pl.multiple_of(jnp.where(turn[2] == 0, 0, part.shape[2]), bands)
+    part_at = pl.multiple_of(jnp.where(turn[2] == 0, whole.shape[2], 0), bands)
+    arriving = [
+        pltpu.make_async_copy(whole, window.at[:, :, pl.ds(whole_at, whole.shape[2])], sems.at[1]),
+        pltpu.make_async_copy(part, window.at[:, :, pl.ds(part_at, part.shape[2])], sems.at[2]),
+    ]
+    for copy in arriving:
+        copy.start()
     front = ids[0] == 0
     kept = planes - 1
     own = jnp.where(front, 1, 0)
@@ -519,21 +542,21 @@
         more[c, 0] = jnp.zeros(more.shape[2:], jnp.float32)
         more[c, planes + 1] = jnp.zeros(more.shape[2:], jnp.float32)
     restore(split, order, planes, more)
-    mortar_planes(turn, whole, part, window, lead, ghost_at)
-    theta_edges(theta_own, left_high, right_low, more)
+    theta_edges(ids[3] % 2 == 0, theta_own, even_theta, odd_theta, more)
+    for copy in arriving:
+        copy.wait()
+    mortar_planes(turn, window, lead, ghost_at)
     axial_faces(ghosts, first, more, lead, terms)
 
-    loading.wait()
     storing = [pltpu.make_async_copy(out.at[c], out_state.at[c], sems.at[c]) for c in range(5)]
     for c in range(5):
-        change = (-0.25 * step_ratio / flux_scale) * (acc[c, 1 : planes + 1] + more[c, 1 : planes + 1])
-        out[c] = 0.75 * base[c] + (0.25 * section[c] + change)
+        out[c] = acc[c, 1 : planes + 1] + flux_factor * more[c, 1 : planes + 1]
         storing[c].start()
     for copy in storing:
         copy.wait()
 
 
-def tail(ids, turn, section, base, acc, split, order, whole, part, theta_own, left_high, right_low):
+def tail(ids, turn, section, acc, split, order, whole, part, theta_own, even_theta, odd_theta):
     _, planes, rows, _ = section.shape
     bands = theta_own.shape[1]
     tiles = rows // bands
@@ -542,7 +565,7 @@
     anywhere = pl.BlockSpec(memory_space=pl.ANY)
     return pl.pallas_call(
         tail_kernel,
-        in_specs=[smem, smem, vmem, anywhere] + [vmem] * 8,
+        in_specs=[smem, smem, vmem, vmem, vmem, vmem, anywhere, anywhere, vmem, vmem, vmem],
         out_specs=anywhere,
         out_shape=jax.ShapeDtypeStruct(section.shape, jnp.float32),
         scratch_shapes=[
@@ -551,12 +574,11 @@
             pltpu.VMEM((22, 2 * ghosts + 3, batch, bands, lanes), jnp.float32),
             pltpu.VMEM((5, ghosts, whole.shape[2] + part.shape[2], lanes), jnp.float32),
             pltpu.VMEM(section.shape, jnp.float32),
-            pltpu.VMEM(section.shape, jnp.float32),
             pltpu.SemaphoreType.DMA((5,)),
         ],
         compiler_params=pltpu.CompilerParams(vmem_limit_bytes=vmem_bytes),
         name="tail",
-    )(ids, turn, section, base, acc, split, order, whole, part, theta_own, left_high, right_low)
+    )(ids, turn, section, acc, split, order, whole, part, theta_own, even_theta, odd_theta)
 
 
 def slab_routes(turns, slabs):
@@ -578,7 +600,7 @@
     slabs = lax.axis_size("theta")
     slab = lax.axis_index("theta")
     parts = lax.axis_size("radial")
-    ids = jnp.stack([lax.axis_index("blk"), lax.axis_index("radial"), parts]).astype(jnp.int32)
+    ids = jnp.stack([lax.axis_index("blk"), lax.axis_index("radial"), parts, slab]).astype(jnp.int32)
     step = rotor_step[0]
     offset = step // 4
     turns = offset // width
@@ -586,20 +608,24 @@
     second_half = start // (width // 2)
     turn = jnp.stack([start % (width // 2), step % 4, second_half])
     base, section = tile_rows(base_state), tile_rows(section_state)
-    section, theta_low, theta_high, theta_own, radial_low, radial_high, whole, part, cells, order = pack(
+    held, even_theta, odd_theta, theta_own, even_radial, odd_radial, whole, part, cells, order = pack(
         ids, turn, section, bands
     )
 
-    def halos(radial_low, radial_high, theta_low, theta_high):
+    def pairs(count, first, closed):
+        ends = range(first, count if closed else count - 1, 2)
+        return [pair for i in ends for pair in ((i, (i + 1) % count), ((i + 1) % count, i))]
+
+    def halos(even_radial, odd_radial, even_theta, odd_theta):
         return (
-            lax.ppermute(radial_high, "radial", [(i, i + 1) for i in range(parts - 1)]),
-            lax.ppermute(radial_low, "radial", [(i + 1, i) for i in range(parts - 1)]),
-            lax.ppermute(theta_high, "theta", [(i, (i + 1) % slabs) for i in range(slabs)]),
-            lax.ppermute(theta_low, "theta", [((i + 1) % slabs, i) for i in range(slabs)]),
+            lax.ppermute(even_radial, "radial", pairs(parts, 0, False)),
+            lax.ppermute(odd_radial, "radial", pairs(parts, 1, False)),
+            lax.ppermute(even_theta, "theta", pairs(slabs, 0, True)),
+            lax.ppermute(odd_theta, "theta", pairs(slabs, 1, True)),
         )
 
     if slabs > most_slabs:
-        low_radial, high_radial, left_high, right_low = halos(radial_low, radial_high, theta_low, theta_high)
+        even_radial, odd_radial, even_theta, odd_theta = halos(even_radial, odd_radial, even_theta, odd_theta)
         facing = lax.ppermute(whole, "blk", [(0, 1), (1, 0)])
         ring = lax.all_gather(facing, "theta", axis=2, tiled=True)
         ring = jnp.concatenate([ring, ring, ring[:, :, : rows // 2]], axis=2)
@@ -607,29 +633,29 @@
         whole = lax.dynamic_slice_in_dim(ring, begin, rows, 2)
         part = lax.dynamic_slice_in_dim(ring, begin + rows, rows // 2, 2)
         turn = turn.at[2].set(0)
-        acc, split = inner(ids, section, cells, bands, low_radial, high_radial)
+        acc, split = inner(ids, held, cells, bands, even_radial, odd_radial, base)
     else:
 
         def branch(case):
             near, far = slab_routes(case // 2 + 1, slabs)
             whole_route, part_route = (near, far) if case % 2 == 0 else (far, near)
 
-            def run(ids, section, cells, whole, part, *ends):
+            def run(ids, held, cells, base, whole, part, *ends):
                 whole = lax.ppermute(whole, ("blk", "theta"), whole_route)
                 part = lax.ppermute(part, ("blk", "theta"), part_route)
-                low_radial, high_radial, left_high, right_low = halos(*ends)
-                acc, split = inner(ids, section, cells, bands, low_radial, high_radial)
-                return acc, split, whole, part, left_high, right_low
+                even_radial, odd_radial, *ends = halos(*ends)
+                acc, split = inner(ids, held, cells, bands, even_radial, odd_radial, base)
+                return acc, split, whole, part, *ends
 
             return run
 
         case = (turns - 1) * 2 + second_half
         branches = [branch(i) for i in range((slabs - 1) * 2)]
-        ends = (radial_low, radial_high, theta_low, theta_high)
-        acc, split, whole, part, left_high, right_low = lax.switch(
-            case, branches, ids, section, cells, whole, part, *ends
+        ends = (even_radial, odd_radial, even_theta, odd_theta)
+        acc, split, whole, part, even_theta, odd_theta = lax.switch(
+            case, branches, ids, held, cells, base, whole, part, *ends
         )
-    out = tail(ids, turn, section, base, acc, split, order, whole, part, theta_own, left_high, right_low)
+    out = tail(ids, turn, section, acc, split, order, whole, part, theta_own, even_theta, odd_theta)
     return from_tile_rows(out, bands)
 
 

time: 48.3 us -> 42.7 us (0.88)
  starting transfers between devices: 12.8 us -> 10.7 us
  waiting for transfers between devices: 4.51 us -> 2.56 us
  Pallas kernels: 28.6 us -> 26.9 us
    ppermute x4, starting transfers between devices: 8.62 us -> 5.27 us  [the longest x1 3.02 us: halos(): lax.ppermute(odd_radial, 'radial', pairs(parts, 1, False))]
    ppermute x1, starting transfers between devices: 0.07 us -> 2.34 us  [run(): part = lax.ppermute(part, ('blk', 'theta'), part_route)]
    ppermute x4, waiting for transfers between devices: 4.51 us -> 2.56 us  [the longest x1 2.55 us: halos(): lax.ppermute(odd_radial, 'radial', pairs(parts, 1, False))]
    ppermute x1, starting transfers between devices: 4.07 us -> 3.12 us  [run(): whole = lax.ppermute(whole, ('blk', 'theta'), whole_route)]
    pallas_call x1, Pallas kernels: 7.28 us -> 6.49 us  [tail(): pl.pallas_call(tail_kernel, in_specs=[smem, smem, vmem, vmem, vmem, vmem,...]
    pallas_call x1, Pallas kernels: 3.58 us -> 2.94 us  [pack(): pl.pallas_call(functools.partial(pack_kernel, bands), in_specs=[smem, sme...]
  transfers between devices with their start and end apart: 6 -> 6, of which waited for: 2 -> 1; matrix products, arithmetic and copies ran while one was open for 0% -> 0% of each run, Pallas kernels for 37% -> 41%
where the time goes in v2:
time: 42.7 us; the launch traced here: 42.5 us
  Pallas kernels  26.9 us (63%)
  starting transfers between devices  10.7 us (25%)
  waiting for transfers between devices  2.56 us (6%)
  local copies, waits for them, and re-layouts  1.21 us (3%)
  between operations  0.77 us (2%)
    pallas_call x1, Pallas kernels, inner(): pl.pallas_call(functools.partial(inner_kernel, bands), in_specs=[pl.Block...  17.5 us
    pallas_call x1, Pallas kernels, tail(): pl.pallas_call(tail_kernel, in_specs=[smem, smem, vmem, vmem, vmem, vmem,...  6.49 us
    ppermute x1, starting transfers between devices, run(): whole = lax.ppermute(whole, ('blk', 'theta'), whole_route)  3.12 us
    ppermute x1, starting transfers between devices, halos(): lax.ppermute(odd_radial, 'radial', pairs(parts, 1, False))  3.02 us
    pallas_call x1, Pallas kernels, pack(): pl.pallas_call(functools.partial(pack_kernel, bands), in_specs=[smem, sme...  2.94 us
    ppermute x1, waiting for transfers between devices, halos(): lax.ppermute(odd_radial, 'radial', pairs(parts, 1, False))  2.55 us
    ppermute x1, starting transfers between devices, run(): part = lax.ppermute(part, ('blk', 'theta'), part_route)  2.34 us
    ppermute x1, starting transfers between devices, halos(): lax.ppermute(odd_theta, 'theta', pairs(slabs, 1, True))  1.29 us
  transfers between devices with their start and end apart: 6, of which 1 were waited for; matrix products, arithmetic and copies ran while one was open for 0% of the time, Pallas kernels for 41%

profile of v2, /device:TPU:1, one launch (start us, length us, event | category | flops | bytes accessed | tf_op | source)
XLA Modules:
  0.0 42.5 jit_solution(12627977158509548421)
XLA Ops:
  0.7 0.1 pad_add_fusion.ids
  0.8 0.1 pad_add_fusion.1.turn
  0.9 0.0 copy-start
  0.9 1.2 %copy-done = f32[5,6,8,1024]{3,2,1,0:T(8,128)S(1)} copy-done((f32[5,6,8,1024]{3,2,1,0:T(8,128)S(1)}, f32[5,6,8,1024]{3,2,1,0:T(8,128)}, u32[]{:S(2)}) %copy-start) | copy-done | bytes 983064
  2.1 2.9 %pack.1 = (f32[5,6,64,128]{3,2,1,0:T(8,128)S(1)}, f32[5,8,128]{2,1,0:T(8,128)S(1)}, f32[5,8,128]{2,1,0:T(8,128)S(1)}, f32[5,8,128]{2,1,0:T(8,128)S(1)}, f32[5,6,...) custom-call(s32[4]{0:T(128)S(1)} %pad_add_fusion.ids, ...), custom_call_target="tpu_custom_call" | custom-call | tf_op jit(solution)/shard_map/pack/pallas_call | solution.py:261
  5.0 0.0 copy-start.1
  5.1 30.9 %conditional.1 = (f32[5,8,64,128]{3,2,1,0:T(8,128)S(1)}, bf16[480,1024]{1,0:T(8,128)(2,1)S(1)}, f32[5,3,64,128]{3,2,1,0:T(8,128)}, f32[5,3,32,128]{3,2,1,0:T(8,1...) conditional(s32[]{:T(128)} %clamp.3, (f32[5,6,3,8,128]{4,3,2,1,0:T(8,128)S(1)}, ...), branch_computations={%region_0.1_spmd, %region_1.2_spmd, %region_2.3_spmd, %region_3.4_... | conditional | flops 117555200 | bytes 9994528 | solution.py:655
  5.1 3.1 %collective-permute-start.14 = (f32[5,3,64,128]{3,2,1,0:T(8,128)S(1)}, f32[5,3,64,128]{3,2,1,0:T(8,128)}, u32[]{:S(2)}, u32[]{:S(2)}) collective-permute-start(f32[5,3,64,128]{3,2,1,0:T(8,128)S(1)} %get-tuple-element.157), channel_id=1, source_target_pairs={{0,20},{4,16},{8,28},{12,24},{16,4},{20,0},{24,12},{28,8},{1,21},{... | collective-permute-start | bytes 1474568 | tf_op jit(solution)/shard_map/cond/branch_2_fun/ppermute | solution.py:644
  8.2 1.0 %collective-permute-start.12 = (f32[5,6,3,8,128]{4,3,2,1,0:T(8,128)S(1)}, f32[5,6,3,8,128]{4,3,2,1,0:T(8,128)S(1)}, u32[]{:S(2)}, u32[]{:S(2)}) collective-permute-start(f32[5,6,3,8,128]{4,3,2,1,0:T(8,128)S(1)} %get-tuple-element.152), channel_id=1, source_target_pairs={{0,1},{1,0},{2,3},{3,2},{4,5},{5,4},{6,7},{7,6},{8,9},{9,8},{10,11... | collective-permute-start | bytes 1105928 | tf_op jit(solution)/shard_map/cond/branch_2_fun/ppermute | solution.py:621
  9.2 3.0 %collective-permute-start.13 = (f32[5,6,3,8,128]{4,3,2,1,0:T(8,128)S(1)}, f32[5,6,3,8,128]{4,3,2,1,0:T(8,128)S(1)}, u32[]{:S(2)}, u32[]{:S(2)}) collective-permute-start(f32[5,6,3,8,128]{4,3,2,1,0:T(8,128)S(1)} %get-tuple-element.153), channel_id=1, source_target_pairs={{1,2},{2,1},{5,6},{6,5},{9,10},{10,9},{13,14},{14,13},{17,18},{18,... | collective-permute-start | bytes 1105928 | tf_op jit(solution)/shard_map/cond/branch_2_fun/ppermute | solution.py:622
  12.2 2.3 %collective-permute-start.15 = (f32[5,3,32,128]{3,2,1,0:T(8,128)S(1)}, f32[5,3,32,128]{3,2,1,0:T(8,128)}, u32[]{:S(2)}, u32[]{:S(2)}) collective-permute-start(f32[5,3,32,128]{3,2,1,0:T(8,128)S(1)} %get-tuple-element.158), channel_id=1, source_target_pairs={{0,24},{4,20},{8,16},{12,28},{16,8},{20,4},{24,0},{28,12},{1,25},{... | collective-permute-start | bytes 737288 | tf_op jit(solution)/shard_map/cond/branch_2_fun/ppermute | solution.py:645
  14.5 0.0 collective-permute-start.16
  14.5 0.0 collective-permute-done.12.even_radial
  14.6 1.3 %collective-permute-start.17 = (f32[5,8,128]{2,1,0:T(8,128)S(1)}, f32[5,8,128]{2,1,0:T(8,128)}, u32[]{:S(2)}, u32[]{:S(2)}) collective-permute-start(f32[5,8,128]{2,1,0:T(8,128)S(1)} %get-tuple-element.160), channel_id=1, source_target_pairs={{4,8},{8,4},{12,0},{0,12},{5,9},{9,5},{13,1},{1,13},{6,10},{10,6},... | collective-permute-start | bytes 61448 | tf_op jit(solution)/shard_map/cond/branch_2_fun/ppermute | solution.py:624
  15.8 2.5 %collective-permute-done.13.odd_radial = f32[5,6,3,8,128]{4,3,2,1,0:T(8,128)S(1)} collective-permute-done((f32[5,6,3,8,128]{4,3,2,1,0:T(8,128)S(1)}, f32[5,6,3,8,128]{4,3,2,1,0:T(8,128)S(1)}, u32[]{:S(2)}, u32[]{:S(2)}) %collective-permute-start.13) | collective-permute-done | bytes 368672 | tf_op jit(solution)/shard_map/cond/branch_2_fun/ppermute | solution.py:622
  18.4 17.5 %inner.8 = (f32[5,8,64,128]{3,2,1,0:T(8,128)S(1)}, bf16[480,1024]{1,0:T(8,128)(2,1)S(1)}) custom-call(s32[4]{0:T(128)S(1)} %get-tuple-element.149.ids, f32[5,6,64,128]{3,2,1,0:T(8,128)S(1)} %get-tuple-element.150.section, f32[5,8,6,8,128]{4,3,2,1,0:T(8,128)S(1)} %get-tuple-element.151.cells, f32[5,6,3,8,128]{4,3,2,1,0:T(8,128)S(1)} %collective-permute-done.12.even_radial, ...), custom_call_target="tpu_custom_call" | custom-call | flops 117555200 | bytes 3932160 | tf_op jit(solution)/shard_map/cond/branch_2_fun/inner/pallas_call | solution.py:433
  35.9 0.0 collective-permute-done.16
  35.9 0.0 collective-permute-done.17
  35.9 0.0 collective-permute-done.15
  35.9 0.0 collective-permute-done.14
  36.0 0.0 copy-done.1
  36.0 6.5 %tail.1 = f32[5,6,64,128]{3,2,1,0:T(8,128)} custom-call(s32[4]{0:T(128)S(1)} %pad_add_fusion.ids, s32[3]{0:T(128)S(1)} %pad_add_fusion.1.turn, f32[5,6,64,128]{3,2,1,0:T(8,128)S(1)} %bitcast.27, f32[5,8,64,128]{3,2,1,0:T(8,128)S(1)} %get-tuple-element.221.acc, bf16[480,1024]{1,0:T(8,128)(2,1)S(1)} %get-tuple-element.222.split, ...), custom_call_target="tpu_custom_call" | custom-call | tf_op jit(solution)/shard_map/tail/pallas_call | solution.py:566
Async XLA Ops:
  0.9 1.2 %copy-start = (f32[5,6,8,1024]{3,2,1,0:T(8,128)S(1)}, f32[5,6,8,1024]{3,2,1,0:T(8,128)}, u32[]{:S(2)}) copy-start(f32[5,6,8,1024]{3,2,1,0:T(8,128)} %param.10) | copy-start | bytes 2949124
  5.0 30.9 %copy-start.1 = (f32[5,6,8,1024]{3,2,1,0:T(8,128)S(1)}, f32[5,6,8,1024]{3,2,1,0:T(8,128)}, u32[]{:S(2)}) copy-start(f32[5,6,8,1024]{3,2,1,0:T(8,128)} %param.10) | copy-start | bytes 2949124
  5.1 30.8 %collective-permute-start.14 = (f32[5,3,64,128]{3,2,1,0:T(8,128)S(1)}, f32[5,3,64,128]{3,2,1,0:T(8,128)}, u32[]{:S(2)}, u32[]{:S(2)}) collective-permute-start(f32[5,3,64,128]{3,2,1,0:T(8,128)S(1)} %get-tuple-element.157), channel_id=1, source_target_pairs={{0,20},{4,16},{8,28},{12,24},{16,4},{20,0},{24,12},{28,8},{1,21},{... | collective-permute-start | bytes 1474568 | tf_op jit(solution)/shard_map/cond/branch_2_fun/ppermute | solution.py:644
  8.2 6.3 %collective-permute-start.12 = (f32[5,6,3,8,128]{4,3,2,1,0:T(8,128)S(1)}, f32[5,6,3,8,128]{4,3,2,1,0:T(8,128)S(1)}, u32[]{:S(2)}, u32[]{:S(2)}) collective-permute-start(f32[5,6,3,8,128]{4,3,2,1,0:T(8,128)S(1)} %get-tuple-element.152), channel_id=1, source_target_pairs={{0,1},{1,0},{2,3},{3,2},{4,5},{5,4},{6,7},{7,6},{8,9},{9,8},{10,11... | collective-permute-start | bytes 1105928 | tf_op jit(solution)/shard_map/cond/branch_2_fun/ppermute | solution.py:621
  9.2 9.2 %collective-permute-start.13 = (f32[5,6,3,8,128]{4,3,2,1,0:T(8,128)S(1)}, f32[5,6,3,8,128]{4,3,2,1,0:T(8,128)S(1)}, u32[]{:S(2)}, u32[]{:S(2)}) collective-permute-start(f32[5,6,3,8,128]{4,3,2,1,0:T(8,128)S(1)} %get-tuple-element.153), channel_id=1, source_target_pairs={{1,2},{2,1},{5,6},{6,5},{9,10},{10,9},{13,14},{14,13},{17,18},{18,... | collective-permute-start | bytes 1105928 | tf_op jit(solution)/shard_map/cond/branch_2_fun/ppermute | solution.py:622
  12.2 23.7 %collective-permute-start.15 = (f32[5,3,32,128]{3,2,1,0:T(8,128)S(1)}, f32[5,3,32,128]{3,2,1,0:T(8,128)}, u32[]{:S(2)}, u32[]{:S(2)}) collective-permute-start(f32[5,3,32,128]{3,2,1,0:T(8,128)S(1)} %get-tuple-element.158), channel_id=1, source_target_pairs={{0,24},{4,20},{8,16},{12,28},{16,8},{20,4},{24,0},{28,12},{1,25},{... | collective-permute-start | bytes 737288 | tf_op jit(solution)/shard_map/cond/branch_2_fun/ppermute | solution.py:645
  14.5 21.4 %collective-permute-start.16 = (f32[5,8,128]{2,1,0:T(8,128)S(1)}, f32[5,8,128]{2,1,0:T(8,128)}, u32[]{:S(2)}, u32[]{:S(2)}) collective-permute-start(f32[5,8,128]{2,1,0:T(8,128)S(1)} %get-tuple-element.159), channel_id=1, source_target_pairs={{0,4},{4,0},{8,12},{12,8},{1,5},{5,1},{9,13},{13,9},{2,6},{6,2},{1... | collective-permute-start | bytes 61448 | tf_op jit(solution)/shard_map/cond/branch_2_fun/ppermute | solution.py:623
  14.6 21.4 %collective-permute-start.17 = (f32[5,8,128]{2,1,0:T(8,128)S(1)}, f32[5,8,128]{2,1,0:T(8,128)}, u32[]{:S(2)}, u32[]{:S(2)}) collective-permute-start(f32[5,8,128]{2,1,0:T(8,128)S(1)} %get-tuple-element.160), channel_id=1, source_target_pairs={{4,8},{8,4},{12,0},{0,12},{5,9},{9,5},{13,1},{1,13},{6,10},{10,6},... | collective-permute-start | bytes 61448 | tf_op jit(solution)/shard_map/cond/branch_2_fun/ppermute | solution.py:624

commit v3 on v2

--- a/solution.py
+++ b/solution.py
@@ -13,7 +13,8 @@
 lanes = 128
 ghosts = 3
 group = 16
-batch = 2
+plane_batch = 3
+tile_batch = 2
 flux_scale = 12.0
 flux_factor = -0.25 * step_ratio / flux_scale
 most_slabs = 8
@@ -154,13 +155,14 @@
 
 def make_order(order):
     tiles = order.shape[0] // lanes
+    one, zero = jnp.ones((lanes, lanes), jnp.bfloat16), jnp.zeros((lanes, lanes), jnp.bfloat16)
     row = lax.broadcasted_iota(jnp.int32, (lanes, lanes), 0)
     column = lax.broadcasted_iota(jnp.int32, (lanes, lanes), 1)
     for t in range(tiles):
         meets = column - row // tiles == t * lanes // tiles
         key = jnp.where(meets, row % tiles, -1).astype(jnp.float32).astype(jnp.bfloat16)
         for j in range(tiles):
-            block = jnp.where(key == j, 1.0, 0.0).astype(jnp.bfloat16)
+            block = jnp.where(key == j, one, zero)
             order[t * lanes : (t + 1) * lanes, j * lanes : (j + 1) * lanes] = block
 
 
@@ -199,16 +201,22 @@
             acc[c, 1 : planes + 1, t * bands : (t + 1) * bands] = part.reshape(planes, bands, lanes)
 
 
+def mortar_turn(step, width):
+    start = lax.rem(lax.div(step, 4), width)
+    return lax.rem(start, width // 2), lax.rem(step, 4), lax.div(start, width // 2)
+
+
 def pack_kernel(
-    bands, ids, turn, section,
+    bands, rotor_step, section,
     held, even_theta, odd_theta, theta_own, even_radial, odd_radial, whole, part, cells, order, split
 ):
     planes, rows = section.shape[1:3]
     tiles = rows // bands
-    facing = jnp.where(ids[0] == 0, planes - ghosts, 0)
+    facing = jnp.where(lax.axis_index("blk") == 0, planes - ghosts, 0)
+    turn = mortar_turn(rotor_step[0], tiles * lanes)
     part_at = pl.multiple_of(turn[2] * part.shape[2], bands)
-    even = ids[1] % 2 == 0
-    even_slab = ids[3] % 2 == 0
+    even = lax.rem(lax.axis_index("radial"), 2) == 0
+    even_slab = lax.rem(lax.axis_index("theta"), 2) == 0
     lane = lane_index((bands, lanes))
 
     def component(c):
@@ -247,7 +255,7 @@
     reorder(section, cells, split, order)
 
 
-def pack(ids, turn, section, bands):
+def pack(rotor_step, section, bands):
     _, planes, rows, _ = section.shape
     smem = pl.BlockSpec(memory_space=pltpu.SMEM)
     vmem = pl.BlockSpec(memory_space=pltpu.VMEM)
@@ -260,31 +268,31 @@
     order = jax.ShapeDtypeStruct((width, width), jnp.bfloat16)
     return pl.pallas_call(
         functools.partial(pack_kernel, bands),
-        in_specs=[smem, smem, vmem],
+        in_specs=[smem, vmem],
         out_specs=[vmem] * 10,
         out_shape=(array(*section.shape), theta, theta, theta, radial, radial, *mortar, cells, order),
         scratch_shapes=[pltpu.VMEM((10 * planes * bands, width), jnp.bfloat16)],
         compiler_params=pltpu.CompilerParams(vmem_limit_bytes=vmem_bytes),
         name="pack",
-    )(ids, turn, section)
+    )(rotor_step, section)
 
 
 def inner_kernel(
-    bands, ids, section, cells, even_radial, odd_radial, base_state, acc, split, lead, terms, fluxes, base, sem
+    bands, section, cells, even_radial, odd_radial, base_state, acc, split, lead, terms, fluxes, base, sem
 ):
     planes = section.shape[1]
     loading = pltpu.make_async_copy(base_state, base, sem)
     loading.start()
-    radial_pass(bands, ids, section, even_radial, odd_radial, acc, lead, terms, fluxes)
+    radial_pass(bands, section, even_radial, odd_radial, acc, lead, terms, fluxes)
     theta_pass(cells, lead, terms, fluxes, split)
-    axial_inner(ids, section, acc, lead, terms)
+    axial_inner(section, acc, lead, terms)
     loading.wait()
     for c in range(5):
         change = flux_factor * acc[c, 1 : planes + 1]
         acc[c, 1 : planes + 1] = 0.75 * base[c] + (0.25 * section[c] + change)
 
 
-def lead_faces(lead, cells, columns, terms, emit):
+def lead_faces(lead, cells, columns, batch, terms, emit):
     def column_group(g):
         p = g * batch
 
@@ -298,24 +306,24 @@
 
         def keep(r, values):
             for n, value in enumerate((*values[1], values[2])):
-                terms[16 + n, r] = value
+                terms[16 + n, r, 0:batch] = value
 
         def interface(r, right):
-            left = (state(r), [terms[16 + n, r] for n in range(5)], terms[21, r])
+            left = (state(r), [terms[16 + n, r, 0:batch] for n in range(5)], terms[21, r, 0:batch])
             for n, value in enumerate(interface_terms(left, right)):
-                terms[n, r] = value
+                terms[n, r, 0:batch] = value
 
         left = cell(0)
         for r in range(5):
             right = cell(r + 1)
             for n, value in enumerate(interface_terms(left, right)):
-                terms[n, r] = value
+                terms[n, r, 0:batch] = value
             left = right
         keep(5, left)
 
         def face(r):
             flux = face_from(
-                lambda n, s: terms[n, r + s],
+                lambda n, s: terms[n, r + s, 0:batch],
                 lambda n: lead[n, r + 2, pl.ds(p, batch)] + lead[n, r + 3, pl.ds(p, batch)],
             )
             emit(r, p, flux)
@@ -330,15 +338,16 @@
 
 def keep_flux(fluxes, r, p, flux):
     for n, value in enumerate(flux):
-        fluxes[n, r, pl.ds(p, batch)] = value
-
-
-def radial_pass(bands, ids, section, even_radial, odd_radial, acc, lead, terms, fluxes):
+        fluxes[n, r, pl.ds(p, plane_batch)] = value
+
+
+def radial_pass(bands, section, even_radial, odd_radial, acc, lead, terms, fluxes):
     planes, rows = section.shape[1:3]
     tiles = rows // bands
-    at_inner = ids[1] == 0
-    at_outer = ids[1] == ids[2] - 1
-    even = ids[1] % 2 == 0
+    index = lax.axis_index("radial")
+    at_inner = index == 0
+    at_outer = index == lax.axis_size("radial") - 1
+    even = lax.rem(index, 2) == 0
 
     def spread(p):
         for n, c in enumerate(radial_order):
@@ -353,7 +362,7 @@
                 lead[n, bands + ghosts + k, p] = jnp.where(at_outer, sign * band[bands - 1 - k], high)
 
     loop(planes, spread)
-    lead_faces(lead, bands + 2 * ghosts, planes, terms, functools.partial(keep_flux, fluxes))
+    lead_faces(lead, bands + 2 * ghosts, planes, plane_batch, terms, functools.partial(keep_flux, fluxes))
 
     def gather(p):
         for n, c in enumerate(radial_order):
@@ -374,7 +383,7 @@
             lead[n, ghosts + tiles + k, 0:planes] = pltpu.roll(cells[n, k], lanes - 1, 2)
 
     loop(5, fill)
-    lead_faces(lead, tiles + 2 * ghosts, planes, terms, functools.partial(keep_flux, fluxes))
+    lead_faces(lead, tiles + 2 * ghosts, planes, plane_batch, terms, functools.partial(keep_flux, fluxes))
     lane = lane_index((planes, bands, lanes))
 
     def changes(n):
@@ -396,19 +405,19 @@
     tiles, bands = lead.shape[2:4]
 
     def emit(i, p, flux):
-        place = pl.ds(pl.multiple_of(p * bands, bands), batch * bands)
+        place = pl.ds(pl.multiple_of(p * bands, bands), tile_batch * bands)
         for c, value in zip(axial_order, flux):
-            value = value.reshape(batch * bands, lanes)
+            value = value.reshape(tile_batch * bands, lanes)
             acc[c, first + i, place] += value
             acc[c, first + i + 1, place] -= value
 
-    lead_faces(lead, count + 5, tiles, terms, emit)
-
-
-def axial_inner(ids, section, acc, lead, terms):
+    lead_faces(lead, count + 5, tiles, tile_batch, terms, emit)
+
+
+def axial_inner(section, acc, lead, terms):
     planes = section.shape[1]
     tiles, bands = lead.shape[2:4]
-    first = jnp.where(ids[0] == 0, 0, ghosts)
+    first = jnp.where(lax.axis_index("blk") == 0, 0, ghosts)
     count = planes + 1 - ghosts
     for c in range(5):
         acc[c, 0] = jnp.zeros(acc.shape[2:], jnp.float32)
@@ -423,7 +432,7 @@
     axial_faces(count, first, acc, lead, terms)
 
 
-def inner(ids, section, cells, bands, even_radial, odd_radial, base):
+def inner(section, cells, bands, even_radial, odd_radial, base):
     _, planes, rows, _ = section.shape
     tiles = rows // bands
     depth = max(bands, tiles) + 2 * ghosts
@@ -432,14 +441,14 @@
     faces = (planes + 1) * tiles + planes * (tiles + bands + 2)
     return pl.pallas_call(
         functools.partial(inner_kernel, bands),
-        in_specs=[pl.BlockSpec(memory_space=pltpu.SMEM)] + [vmem] * 4 + [pl.BlockSpec(memory_space=pl.ANY)],
+        in_specs=[vmem] * 4 + [pl.BlockSpec(memory_space=pl.ANY)],
         out_shape=(
             jax.ShapeDtypeStruct((5, planes + 2, rows, lanes), jnp.float32),
             jax.ShapeDtypeStruct((10 * planes * bands, tiles * lanes), jnp.bfloat16),
         ),
         scratch_shapes=[
             pltpu.VMEM((5, depth, across, 8, lanes), jnp.float32),
-            pltpu.VMEM((22, depth + 1, batch, 8, lanes), jnp.float32),
+            pltpu.VMEM((22, depth + 1, max(plane_batch, tile_batch), 8, lanes), jnp.float32),
             pltpu.VMEM((5, depth - 5, planes, 8, lanes), jnp.float32),
             pltpu.VMEM(section.shape, jnp.float32),
             pltpu.SemaphoreType.DMA(()),
@@ -449,7 +458,7 @@
             flops=faces * 8 * lanes * 700, bytes_accessed=section.size * 16, transcendentals=faces * 8 * lanes * 30
         ),
         name="inner",
-    )(ids, section, cells, even_radial, odd_radial, base)
+    )(section, cells, even_radial, odd_radial, base)
 
 
 def mortar_planes(turn, window, lead, at):
@@ -512,20 +521,22 @@
 
 
 def tail_kernel(
-    ids, turn, section, acc, split, order, whole, part, theta_own, even_theta, odd_theta, out_state,
+    gathered, rotor_step, section, acc, split, order, whole, part, theta_own, even_theta, odd_theta, out_state,
     more, lead, terms, window, out, sems
 ):
     planes = section.shape[1]
     tiles, bands = lead.shape[2:4]
-    whole_at = pl.multiple_of(jnp.where(turn[2] == 0, 0, part.shape[2]), bands)
-    part_at = pl.multiple_of(jnp.where(turn[2] == 0, whole.shape[2], 0), bands)
+    turn = mortar_turn(rotor_step[0], tiles * lanes)
+    swapped = (turn[2] == 1) & (not gathered)
+    whole_at = pl.multiple_of(jnp.where(swapped, part.shape[2], 0), bands)
+    part_at = pl.multiple_of(jnp.where(swapped, 0, whole.shape[2]), bands)
     arriving = [
         pltpu.make_async_copy(whole, window.at[:, :, pl.ds(whole_at, whole.shape[2])], sems.at[1]),
         pltpu.make_async_copy(part, window.at[:, :, pl.ds(part_at, part.shape[2])], sems.at[2]),
     ]
     for copy in arriving:
         copy.start()
-    front = ids[0] == 0
+    front = lax.axis_index("blk") == 0
     kept = planes - 1
     own = jnp.where(front, 1, 0)
     own_at = jnp.where(front, 0, ghosts)
@@ -542,7 +553,7 @@
         more[c, 0] = jnp.zeros(more.shape[2:], jnp.float32)
         more[c, planes + 1] = jnp.zeros(more.shape[2:], jnp.float32)
     restore(split, order, planes, more)
-    theta_edges(ids[3] % 2 == 0, theta_own, even_theta, odd_theta, more)
+    theta_edges(lax.rem(lax.axis_index("theta"), 2) == 0, theta_own, even_theta, odd_theta, more)
     for copy in arriving:
         copy.wait()
     mortar_planes(turn, window, lead, ghost_at)
@@ -556,7 +567,7 @@
         copy.wait()
 
 
-def tail(ids, turn, section, acc, split, order, whole, part, theta_own, even_theta, odd_theta):
+def tail(gathered, rotor_step, section, acc, split, order, whole, part, theta_own, even_theta, odd_theta):
     _, planes, rows, _ = section.shape
     bands = theta_own.shape[1]
     tiles = rows // bands
@@ -564,21 +575,21 @@
     vmem = pl.BlockSpec(memory_space=pltpu.VMEM)
     anywhere = pl.BlockSpec(memory_space=pl.ANY)
     return pl.pallas_call(
-        tail_kernel,
-        in_specs=[smem, smem, vmem, vmem, vmem, vmem, anywhere, anywhere, vmem, vmem, vmem],
+        functools.partial(tail_kernel, gathered),
+        in_specs=[smem, vmem, vmem, vmem, vmem, anywhere, anywhere, vmem, vmem, vmem],
         out_specs=anywhere,
         out_shape=jax.ShapeDtypeStruct(section.shape, jnp.float32),
         scratch_shapes=[
             pltpu.VMEM(acc.shape, jnp.float32),
             pltpu.VMEM((5, planes - 1 + ghosts, tiles, bands, lanes), jnp.float32),
-            pltpu.VMEM((22, 2 * ghosts + 3, batch, bands, lanes), jnp.float32),
+            pltpu.VMEM((22, 2 * ghosts + 3, tile_batch, bands, lanes), jnp.float32),
             pltpu.VMEM((5, ghosts, whole.shape[2] + part.shape[2], lanes), jnp.float32),
             pltpu.VMEM(section.shape, jnp.float32),
             pltpu.SemaphoreType.DMA((5,)),
         ],
         compiler_params=pltpu.CompilerParams(vmem_limit_bytes=vmem_bytes),
         name="tail",
-    )(ids, turn, section, acc, split, order, whole, part, theta_own, even_theta, odd_theta)
+    )(rotor_step, section, acc, split, order, whole, part, theta_own, even_theta, odd_theta)
 
 
 def slab_routes(turns, slabs):
@@ -600,16 +611,13 @@
     slabs = lax.axis_size("theta")
     slab = lax.axis_index("theta")
     parts = lax.axis_size("radial")
-    ids = jnp.stack([lax.axis_index("blk"), lax.axis_index("radial"), parts, slab]).astype(jnp.int32)
-    step = rotor_step[0]
-    offset = step // 4
-    turns = offset // width
-    start = offset % width
-    second_half = start // (width // 2)
-    turn = jnp.stack([start % (width // 2), step % 4, second_half])
+    offset = lax.div(rotor_step[0], 4)
+    turns = lax.div(offset, width)
+    second_half = lax.div(lax.rem(offset, width), width // 2)
+    gathered = slabs > most_slabs
     base, section = tile_rows(base_state), tile_rows(section_state)
     held, even_theta, odd_theta, theta_own, even_radial, odd_radial, whole, part, cells, order = pack(
-        ids, turn, section, bands
+        rotor_step, section, bands
     )
 
     def pairs(count, first, closed):
@@ -624,7 +632,7 @@
             lax.ppermute(odd_theta, "theta", pairs(slabs, 1, True)),
         )
 
-    if slabs > most_slabs:
+    if gathered:
         even_radial, odd_radial, even_theta, odd_theta = halos(even_radial, odd_radial, even_theta, odd_theta)
         facing = lax.ppermute(whole, "blk", [(0, 1), (1, 0)])
         ring = lax.all_gather(facing, "theta", axis=2, tiled=True)
@@ -632,19 +640,18 @@
         begin = (turns - 1 - slab) % slabs * rows + second_half * (rows // 2)
         whole = lax.dynamic_slice_in_dim(ring, begin, rows, 2)
         part = lax.dynamic_slice_in_dim(ring, begin + rows, rows // 2, 2)
-        turn = turn.at[2].set(0)
-        acc, split = inner(ids, held, cells, bands, even_radial, odd_radial, base)
+        acc, split = inner(held, cells, bands, even_radial, odd_radial, base)
     else:
 
         def branch(case):
             near, far = slab_routes(case // 2 + 1, slabs)
             whole_route, part_route = (near, far) if case % 2 == 0 else (far, near)
 
-            def run(ids, held, cells, base, whole, part, *ends):
+            def run(held, cells, base, whole, part, *ends):
                 whole = lax.ppermute(whole, ("blk", "theta"), whole_route)
                 part = lax.ppermute(part, ("blk", "theta"), part_route)
                 even_radial, odd_radial, *ends = halos(*ends)
-                acc, split = inner(ids, held, cells, bands, even_radial, odd_radial, base)
+                acc, split = inner(held, cells, bands, even_radial, odd_radial, base)
                 return acc, split, whole, part, *ends
 
             return run
@@ -653,9 +660,9 @@
         branches = [branch(i) for i in range((slabs - 1) * 2)]
         ends = (even_radial, odd_radial, even_theta, odd_theta)
         acc, split, whole, part, even_theta, odd_theta = lax.switch(
-            case, branches, ids, held, cells, base, whole, part, *ends
+            case, branches, held, cells, base, whole, part, *ends
         )
-    out = tail(ids, turn, section, acc, split, order, whole, part, theta_own, even_theta, odd_theta)
+    out = tail(gathered, rotor_step, section, acc, split, order, whole, part, theta_own, even_theta, odd_theta)
     return from_tile_rows(out, bands)
 
 

time: 42.7 us -> 40.5 us (0.948); the launches traced: 42.5 us -> 39.7 us
  Pallas kernels: 26.9 us -> 24.4 us
    pallas_call x3, Pallas kernels: 26.9 us -> 24.4 us  [the longest x1 16.5 us: inner(): pl.pallas_call(functools.partial(inner_kernel, bands), in_specs=[vmem] *...]
  transfers between devices with their start and end apart: 6 -> 6, of which waited for: 1 -> 1; matrix products, arithmetic and copies ran while one was open for 0% -> 0% of each run, Pallas kernels for 41% -> 42%
where the time goes in v3:
time: 40.5 us; the launch traced here: 39.7 us
  Pallas kernels  24.4 us (60%)
  starting transfers between devices  10.7 us (26%)
  waiting for transfers between devices  2.56 us (6%)
  local copies, waits for them, and re-layouts  1.2 us (3%)
  between operations  0.71 us (2%)
    pallas_call x1, Pallas kernels, inner(): pl.pallas_call(functools.partial(inner_kernel, bands), in_specs=[vmem] *...  16.5 us
    pallas_call x1, Pallas kernels, tail(): pl.pallas_call(functools.partial(tail_kernel, gathered), in_specs=[smem,...  6.46 us
    ppermute x1, starting transfers between devices, run(): whole = lax.ppermute(whole, ('blk', 'theta'), whole_route)  3.12 us
    ppermute x1, starting transfers between devices, halos(): lax.ppermute(odd_radial, 'radial', pairs(parts, 1, False))  3.02 us
    ppermute x1, waiting for transfers between devices, halos(): lax.ppermute(odd_radial, 'radial', pairs(parts, 1, False))  2.55 us
    ppermute x1, starting transfers between devices, run(): part = lax.ppermute(part, ('blk', 'theta'), part_route)  2.34 us
    pallas_call x1, Pallas kernels, pack(): pl.pallas_call(functools.partial(pack_kernel, bands), in_specs=[smem, vme...  1.49 us
    ppermute x1, starting transfers between devices, halos(): lax.ppermute(odd_theta, 'theta', pairs(slabs, 1, True))  1.29 us
  transfers between devices with their start and end apart: 6, of which 1 were waited for; matrix products, arithmetic and copies ran while one was open for 0% of the time, Pallas kernels for 42%

profile of v3, /device:TPU:1, one launch (start us, length us, event | category | flops | bytes accessed | tf_op | source)
XLA Modules:
  0.0 39.7 jit_solution(6819989321833027609)
XLA Ops:
  0.7 0.0 copy-start
  0.7 1.2 %copy-done = f32[5,6,8,1024]{3,2,1,0:T(8,128)S(1)} copy-done((f32[5,6,8,1024]{3,2,1,0:T(8,128)S(1)}, f32[5,6,8,1024]{3,2,1,0:T(8,128)}, u32[]{:S(2)}) %copy-start) | copy-done | bytes 983064
  1.9 1.5 %pack.1 = (f32[5,6,64,128]{3,2,1,0:T(8,128)S(1)}, f32[5,8,128]{2,1,0:T(8,128)S(1)}, f32[5,8,128]{2,1,0:T(8,128)S(1)}, f32[5,8,128]{2,1,0:T(8,128)S(1)}, f32[5,6,...) custom-call(s32[1]{0:T(128)} %copy.40.rotor_step, ...), custom_call_target="tpu_custom_call" | custom-call | tf_op jit(solution)/shard_map/pack/pallas_call | solution.py:269
  3.4 0.0 copy-start.1
  3.4 29.9 %conditional.1 = (f32[5,8,64,128]{3,2,1,0:T(8,128)S(1)}, bf16[480,1024]{1,0:T(8,128)(2,1)S(1)}, f32[5,3,64,128]{3,2,1,0:T(8,128)}, f32[5,3,32,128]{3,2,1,0:T(8,1...) conditional(s32[]{:T(128)} %clamp.3, (f32[5,6,3,8,128]{4,3,2,1,0:T(8,128)S(1)}, ...), branch_computations={%region_0.0_spmd, %region_1.0_spmd, %region_2.0_spmd, %region_3.0_... | conditional | flops 117555200 | bytes 9994528 | solution.py:662
  3.4 3.1 %collective-permute-start.14 = (f32[5,3,64,128]{3,2,1,0:T(8,128)S(1)}, f32[5,3,64,128]{3,2,1,0:T(8,128)}, u32[]{:S(2)}, u32[]{:S(2)}) collective-permute-start(f32[5,3,64,128]{3,2,1,0:T(8,128)S(1)} %get-tuple-element.142), channel_id=1, source_target_pairs={{0,20},{4,16},{8,28},{12,24},{16,4},{20,0},{24,12},{28,8},{1,21},{... | collective-permute-start | bytes 1474568 | tf_op jit(solution)/shard_map/cond/branch_2_fun/ppermute | solution.py:651
  6.5 1.0 %collective-permute-start.12 = (f32[5,6,3,8,128]{4,3,2,1,0:T(8,128)S(1)}, f32[5,6,3,8,128]{4,3,2,1,0:T(8,128)S(1)}, u32[]{:S(2)}, u32[]{:S(2)}) collective-permute-start(f32[5,6,3,8,128]{4,3,2,1,0:T(8,128)S(1)} %get-tuple-element.137), channel_id=1, source_target_pairs={{0,1},{1,0},{2,3},{3,2},{4,5},{5,4},{6,7},{7,6},{8,9},{9,8},{10,11... | collective-permute-start | bytes 1105928 | tf_op jit(solution)/shard_map/cond/branch_2_fun/ppermute | solution.py:629
  7.5 3.0 %collective-permute-start.13 = (f32[5,6,3,8,128]{4,3,2,1,0:T(8,128)S(1)}, f32[5,6,3,8,128]{4,3,2,1,0:T(8,128)S(1)}, u32[]{:S(2)}, u32[]{:S(2)}) collective-permute-start(f32[5,6,3,8,128]{4,3,2,1,0:T(8,128)S(1)} %get-tuple-element.138), channel_id=1, source_target_pairs={{1,2},{2,1},{5,6},{6,5},{9,10},{10,9},{13,14},{14,13},{17,18},{18,... | collective-permute-start | bytes 1105928 | tf_op jit(solution)/shard_map/cond/branch_2_fun/ppermute | solution.py:630
  10.5 2.3 %collective-permute-start.15 = (f32[5,3,32,128]{3,2,1,0:T(8,128)S(1)}, f32[5,3,32,128]{3,2,1,0:T(8,128)}, u32[]{:S(2)}, u32[]{:S(2)}) collective-permute-start(f32[5,3,32,128]{3,2,1,0:T(8,128)S(1)} %get-tuple-element.143), channel_id=1, source_target_pairs={{0,24},{4,20},{8,16},{12,28},{16,8},{20,4},{24,0},{28,12},{1,25},{... | collective-permute-start | bytes 737288 | tf_op jit(solution)/shard_map/cond/branch_2_fun/ppermute | solution.py:652
  12.9 0.0 collective-permute-start.16
  12.9 0.0 collective-permute-done.12.even_radial
  12.9 1.3 %collective-permute-start.17 = (f32[5,8,128]{2,1,0:T(8,128)S(1)}, f32[5,8,128]{2,1,0:T(8,128)}, u32[]{:S(2)}, u32[]{:S(2)}) collective-permute-start(f32[5,8,128]{2,1,0:T(8,128)S(1)} %get-tuple-element.145), channel_id=1, source_target_pairs={{4,8},{8,4},{12,0},{0,12},{5,9},{9,5},{13,1},{1,13},{6,10},{10,6},... | collective-permute-start | bytes 61448 | tf_op jit(solution)/shard_map/cond/branch_2_fun/ppermute | solution.py:632
  14.2 2.5 %collective-permute-done.13.odd_radial = f32[5,6,3,8,128]{4,3,2,1,0:T(8,128)S(1)} collective-permute-done((f32[5,6,3,8,128]{4,3,2,1,0:T(8,128)S(1)}, f32[5,6,3,8,128]{4,3,2,1,0:T(8,128)S(1)}, u32[]{:S(2)}, u32[]{:S(2)}) %collective-permute-start.13) | collective-permute-done | bytes 368672 | tf_op jit(solution)/shard_map/cond/branch_2_fun/ppermute | solution.py:630
  16.7 16.5 %inner.8 = (f32[5,8,64,128]{3,2,1,0:T(8,128)S(1)}, bf16[480,1024]{1,0:T(8,128)(2,1)S(1)}) custom-call(f32[5,6,64,128]{3,2,1,0:T(8,128)S(1)} %get-tuple-element.135.section, f32[5,8,6,8,128]{4,3,2,1,0:T(8,128)S(1)} %get-tuple-element.136.cells, f32[5,6,3,8,128]{4,3,2,1,0:T(8,128)S(1)} %collective-permute-done.12.even_radial, ...), custom_call_target="tpu_custom_call" | custom-call | flops 117555200 | bytes 3932160 | tf_op jit(solution)/shard_map/cond/branch_2_fun/inner/pallas_call | solution.py:442
  33.2 0.0 collective-permute-done.16
  33.2 0.0 collective-permute-done.17
  33.2 0.0 collective-permute-done.15
  33.3 0.0 collective-permute-done.14
  33.3 0.0 copy-done.1
  33.3 6.5 %tail.1 = f32[5,6,64,128]{3,2,1,0:T(8,128)} custom-call(s32[1]{0:T(128)} %copy.40.rotor_step, f32[5,6,64,128]{3,2,1,0:T(8,128)S(1)} %bitcast.20, f32[5,8,64,128]{3,2,1,0:T(8,128)S(1)} %get-tuple-element.203.acc, bf16[480,1024]{1,0:T(8,128)(2,1)S(1)} %get-tuple-element.204.split, bf16[1024,1024]{1,0:T(8,128)(2,1)S(1)} %get-tuple-element.205.order, ...), custom_call_target="tpu_custom_call" | custom-call | tf_op jit(solution)/shard_map/tail/pallas_call | solution.py:577
Async XLA Ops:
  0.7 1.2 %copy-start = (f32[5,6,8,1024]{3,2,1,0:T(8,128)S(1)}, f32[5,6,8,1024]{3,2,1,0:T(8,128)}, u32[]{:S(2)}) copy-start(f32[5,6,8,1024]{3,2,1,0:T(8,128)} %param.10) | copy-start | bytes 2949124
  3.4 29.9 %copy-start.1 = (f32[5,6,8,1024]{3,2,1,0:T(8,128)S(1)}, f32[5,6,8,1024]{3,2,1,0:T(8,128)}, u32[]{:S(2)}) copy-start(f32[5,6,8,1024]{3,2,1,0:T(8,128)} %param.10) | copy-start | bytes 2949124
  3.4 29.8 %collective-permute-start.14 = (f32[5,3,64,128]{3,2,1,0:T(8,128)S(1)}, f32[5,3,64,128]{3,2,1,0:T(8,128)}, u32[]{:S(2)}, u32[]{:S(2)}) collective-permute-start(f32[5,3,64,128]{3,2,1,0:T(8,128)S(1)} %get-tuple-element.142), channel_id=1, source_target_pairs={{0,20},{4,16},{8,28},{12,24},{16,4},{20,0},{24,12},{28,8},{1,21},{... | collective-permute-start | bytes 1474568 | tf_op jit(solution)/shard_map/cond/branch_2_fun/ppermute | solution.py:651
  6.5 6.3 %collective-permute-start.12 = (f32[5,6,3,8,128]{4,3,2,1,0:T(8,128)S(1)}, f32[5,6,3,8,128]{4,3,2,1,0:T(8,128)S(1)}, u32[]{:S(2)}, u32[]{:S(2)}) collective-permute-start(f32[5,6,3,8,128]{4,3,2,1,0:T(8,128)S(1)} %get-tuple-element.137), channel_id=1, source_target_pairs={{0,1},{1,0},{2,3},{3,2},{4,5},{5,4},{6,7},{7,6},{8,9},{9,8},{10,11... | collective-permute-start | bytes 1105928 | tf_op jit(solution)/shard_map/cond/branch_2_fun/ppermute | solution.py:629
  7.5 9.2 %collective-permute-start.13 = (f32[5,6,3,8,128]{4,3,2,1,0:T(8,128)S(1)}, f32[5,6,3,8,128]{4,3,2,1,0:T(8,128)S(1)}, u32[]{:S(2)}, u32[]{:S(2)}) collective-permute-start(f32[5,6,3,8,128]{4,3,2,1,0:T(8,128)S(1)} %get-tuple-element.138), channel_id=1, source_target_pairs={{1,2},{2,1},{5,6},{6,5},{9,10},{10,9},{13,14},{14,13},{17,18},{18,... | collective-permute-start | bytes 1105928 | tf_op jit(solution)/shard_map/cond/branch_2_fun/ppermute | solution.py:630
  10.5 22.7 %collective-permute-start.15 = (f32[5,3,32,128]{3,2,1,0:T(8,128)S(1)}, f32[5,3,32,128]{3,2,1,0:T(8,128)}, u32[]{:S(2)}, u32[]{:S(2)}) collective-permute-start(f32[5,3,32,128]{3,2,1,0:T(8,128)S(1)} %get-tuple-element.143), channel_id=1, source_target_pairs={{0,24},{4,20},{8,16},{12,28},{16,8},{20,4},{24,0},{28,12},{1,25},{... | collective-permute-start | bytes 737288 | tf_op jit(solution)/shard_map/cond/branch_2_fun/ppermute | solution.py:652
  12.9 20.3 %collective-permute-start.16 = (f32[5,8,128]{2,1,0:T(8,128)S(1)}, f32[5,8,128]{2,1,0:T(8,128)}, u32[]{:S(2)}, u32[]{:S(2)}) collective-permute-start(f32[5,8,128]{2,1,0:T(8,128)S(1)} %get-tuple-element.144), channel_id=1, source_target_pairs={{0,4},{4,0},{8,12},{12,8},{1,5},{5,1},{9,13},{13,9},{2,6},{6,2},{1... | collective-permute-start | bytes 61448 | tf_op jit(solution)/shard_map/cond/branch_2_fun/ppermute | solution.py:631
  12.9 20.4 %collective-permute-start.17 = (f32[5,8,128]{2,1,0:T(8,128)S(1)}, f32[5,8,128]{2,1,0:T(8,128)}, u32[]{:S(2)}, u32[]{:S(2)}) collective-permute-start(f32[5,8,128]{2,1,0:T(8,128)S(1)} %get-tuple-element.145), channel_id=1, source_target_pairs={{4,8},{8,4},{12,0},{0,12},{5,9},{9,5},{13,1},{1,13},{6,10},{10,6},... | collective-permute-start | bytes 61448 | tf_op jit(solution)/shard_map/cond/branch_2_fun/ppermute | solution.py:632

commit v4 on v3

--- a/solution.py
+++ b/solution.py
@@ -327,11 +327,17 @@
                 lambda n: lead[n, r + 2, pl.ds(p, batch)] + lead[n, r + 3, pl.ds(p, batch)],
             )
             emit(r, p, flux)
+            if isinstance(r, int) and r + 6 == cells:
+                return
             right = cell(jnp.minimum(r + 6, cells - 1))
             interface(r + 5, right)
             keep(r + 6, right)
 
-        loop(cells - 5, face)
+        if cells - 5 > ghosts:
+            loop(cells - 5, face)
+        else:
+            for r in range(cells - 5):
+                face(r)
 
     loop(columns // batch, column_group)
 

time: 40.5 us -> 39.9 us (0.985)
  the two profiles are of different devices: /device:TPU:1 before, /device:TPU:9 now
where the time goes in v4:
time: 39.9 us; the launch traced here: 39.7 us
  Pallas kernels  24.2 us (61%)
  starting transfers between devices  8.78 us (22%)
  waiting for transfers between devices  4.69 us (12%)
  local copies, waits for them, and re-layouts  1.2 us (3%)
  between operations  0.71 us (2%)
    pallas_call x1, Pallas kernels, inner(): pl.pallas_call(functools.partial(inner_kernel, bands), in_specs=[vmem] *...  16.5 us
    pallas_call x1, Pallas kernels, tail(): pl.pallas_call(functools.partial(tail_kernel, gathered), in_specs=[smem,...  6.27 us
    ppermute x1, waiting for transfers between devices, halos(): lax.ppermute(odd_radial, 'radial', pairs(parts, 1, False))  4.68 us
    ppermute x1, starting transfers between devices, run(): whole = lax.ppermute(whole, ('blk', 'theta'), whole_route)  3.3 us
    ppermute x1, starting transfers between devices, halos(): lax.ppermute(odd_radial, 'radial', pairs(parts, 1, False))  3.02 us
    pallas_call x1, Pallas kernels, pack(): pl.pallas_call(functools.partial(pack_kernel, bands), in_specs=[smem, vme...  1.49 us
    ppermute x1, starting transfers between devices, halos(): lax.ppermute(even_theta, 'theta', pairs(slabs, 0, True))  1.42 us
    unnamed x4, local copies, waits for them, and re-layouts  1.2 us
  transfers between devices with their start and end apart: 6, of which 1 were waited for; matrix products, arithmetic and copies ran while one was open for 0% of the time, Pallas kernels for 42%

profile of v4, /device:TPU:9, one launch (start us, length us, event | category | flops | bytes accessed | tf_op | source)
XLA Modules:
  0.0 39.7 jit_solution(1289119284100436512)
XLA Ops:
  0.7 0.0 copy-start
  0.7 1.2 %copy-done = f32[5,6,8,1024]{3,2,1,0:T(8,128)S(1)} copy-done((f32[5,6,8,1024]{3,2,1,0:T(8,128)S(1)}, f32[5,6,8,1024]{3,2,1,0:T(8,128)}, u32[]{:S(2)}) %copy-start) | copy-done | bytes 983064
  1.9 1.5 %pack.1 = (f32[5,6,64,128]{3,2,1,0:T(8,128)S(1)}, f32[5,8,128]{2,1,0:T(8,128)S(1)}, f32[5,8,128]{2,1,0:T(8,128)S(1)}, f32[5,8,128]{2,1,0:T(8,128)S(1)}, f32[5,6,...) custom-call(s32[1]{0:T(128)} %copy.40.rotor_step, ...), custom_call_target="tpu_custom_call" | custom-call | tf_op jit(solution)/shard_map/pack/pallas_call | solution.py:269
  3.4 0.0 copy-start.1
  3.4 30.1 %conditional.1 = (f32[5,8,64,128]{3,2,1,0:T(8,128)S(1)}, bf16[480,1024]{1,0:T(8,128)(2,1)S(1)}, f32[5,3,64,128]{3,2,1,0:T(8,128)}, f32[5,3,32,128]{3,2,1,0:T(8,1...) conditional(s32[]{:T(128)} %clamp.3, (f32[5,6,3,8,128]{4,3,2,1,0:T(8,128)S(1)}, ...), branch_computations={%region_0.0_spmd, %region_1.0_spmd, %region_2.0_spmd, %region_3.0_... | conditional | flops 117555200 | bytes 9994528 | solution.py:668
  3.4 3.3 %collective-permute-start.2 = (f32[5,3,64,128]{3,2,1,0:T(8,128)S(1)}, f32[5,3,64,128]{3,2,1,0:T(8,128)}, u32[]{:S(2)}, u32[]{:S(2)}) collective-permute-start(f32[5,3,64,128]{3,2,1,0:T(8,128)S(1)} %get-tuple-element.120), channel_id=1, source_target_pairs={{0,16},{4,28},{8,24},{12,20},{16,0},{20,12},{24,8},{28,4},{1,17},{... | collective-permute-start | bytes 1474568 | tf_op jit(solution)/shard_map/cond/branch_0_fun/ppermute | solution.py:657
  6.7 1.0 %collective-permute-start = (f32[5,6,3,8,128]{4,3,2,1,0:T(8,128)S(1)}, f32[5,6,3,8,128]{4,3,2,1,0:T(8,128)S(1)}, u32[]{:S(2)}, u32[]{:S(2)}) collective-permute-start(f32[5,6,3,8,128]{4,3,2,1,0:T(8,128)S(1)} %get-tuple-element.115), channel_id=1, source_target_pairs={{0,1},{1,0},{2,3},{3,2},{4,5},{5,4},{6,7},{7,6},{8,9},{9,8},{10,11... | collective-permute-start | bytes 1105928 | tf_op jit(solution)/shard_map/cond/branch_0_fun/ppermute | solution.py:635
  7.7 3.0 %collective-permute-start.1 = (f32[5,6,3,8,128]{4,3,2,1,0:T(8,128)S(1)}, f32[5,6,3,8,128]{4,3,2,1,0:T(8,128)S(1)}, u32[]{:S(2)}, u32[]{:S(2)}) collective-permute-start(f32[5,6,3,8,128]{4,3,2,1,0:T(8,128)S(1)} %get-tuple-element.116), channel_id=1, source_target_pairs={{1,2},{2,1},{5,6},{6,5},{9,10},{10,9},{13,14},{14,13},{17,18},{18,... | collective-permute-start | bytes 1105928 | tf_op jit(solution)/shard_map/cond/branch_0_fun/ppermute | solution.py:636
  10.7 0.1 collective-permute-start.3
  10.8 1.4 %collective-permute-start.4 = (f32[5,8,128]{2,1,0:T(8,128)S(1)}, f32[5,8,128]{2,1,0:T(8,128)}, u32[]{:S(2)}, u32[]{:S(2)}) collective-permute-start(f32[5,8,128]{2,1,0:T(8,128)S(1)} %get-tuple-element.122), channel_id=1, source_target_pairs={{0,4},{4,0},{8,12},{12,8},{1,5},{5,1},{9,13},{13,9},{2,6},{6,2},{1... | collective-permute-start | bytes 61448 | tf_op jit(solution)/shard_map/cond/branch_0_fun/ppermute | solution.py:637
  12.2 0.0 collective-permute-done.even_radial
  12.2 0.0 collective-permute-start.5
  12.2 4.7 %collective-permute-done.1.odd_radial = f32[5,6,3,8,128]{4,3,2,1,0:T(8,128)S(1)} collective-permute-done((f32[5,6,3,8,128]{4,3,2,1,0:T(8,128)S(1)}, f32[5,6,3,8,128]{4,3,2,1,0:T(8,128)S(1)}, u32[]{:S(2)}, u32[]{:S(2)}) %collective-permute-start.1) | collective-permute-done | bytes 368672 | tf_op jit(solution)/shard_map/cond/branch_0_fun/ppermute | solution.py:636
  16.9 16.5 %inner.6 = (f32[5,8,64,128]{3,2,1,0:T(8,128)S(1)}, bf16[480,1024]{1,0:T(8,128)(2,1)S(1)}) custom-call(f32[5,6,64,128]{3,2,1,0:T(8,128)S(1)} %get-tuple-element.113.section, f32[5,8,6,8,128]{4,3,2,1,0:T(8,128)S(1)} %get-tuple-element.114.cells, f32[5,6,3,8,128]{4,3,2,1,0:T(8,128)S(1)} %collective-permute-done.even_radial, ...), custom_call_target="tpu_custom_call" | custom-call | flops 117555200 | bytes 3932160 | tf_op jit(solution)/shard_map/cond/branch_0_fun/inner/pallas_call | solution.py:448
  33.4 0.0 collective-permute-done.4
  33.4 0.0 collective-permute-done.5
  33.4 0.0 collective-permute-done.3
  33.4 0.0 collective-permute-done.2
  33.4 0.0 copy-done.1
  33.5 6.3 %tail.1 = f32[5,6,64,128]{3,2,1,0:T(8,128)} custom-call(s32[1]{0:T(128)} %copy.40.rotor_step, f32[5,6,64,128]{3,2,1,0:T(8,128)S(1)} %bitcast.20, f32[5,8,64,128]{3,2,1,0:T(8,128)S(1)} %get-tuple-element.203.acc, bf16[480,1024]{1,0:T(8,128)(2,1)S(1)} %get-tuple-element.204.split, bf16[1024,1024]{1,0:T(8,128)(2,1)S(1)} %get-tuple-element.205.order, ...), custom_call_target="tpu_custom_call" | custom-call | tf_op jit(solution)/shard_map/tail/pallas_call | solution.py:583
Async XLA Ops:
  0.7 1.2 %copy-start = (f32[5,6,8,1024]{3,2,1,0:T(8,128)S(1)}, f32[5,6,8,1024]{3,2,1,0:T(8,128)}, u32[]{:S(2)}) copy-start(f32[5,6,8,1024]{3,2,1,0:T(8,128)} %param.10) | copy-start | bytes 2949124
  3.4 30.1 %copy-start.1 = (f32[5,6,8,1024]{3,2,1,0:T(8,128)S(1)}, f32[5,6,8,1024]{3,2,1,0:T(8,128)}, u32[]{:S(2)}) copy-start(f32[5,6,8,1024]{3,2,1,0:T(8,128)} %param.10) | copy-start | bytes 2949124
  3.4 30.0 %collective-permute-start.2 = (f32[5,3,64,128]{3,2,1,0:T(8,128)S(1)}, f32[5,3,64,128]{3,2,1,0:T(8,128)}, u32[]{:S(2)}, u32[]{:S(2)}) collective-permute-start(f32[5,3,64,128]{3,2,1,0:T(8,128)S(1)} %get-tuple-element.120), channel_id=1, source_target_pairs={{0,16},{4,28},{8,24},{12,20},{16,0},{20,12},{24,8},{28,4},{1,17},{... | collective-permute-start | bytes 1474568 | tf_op jit(solution)/shard_map/cond/branch_0_fun/ppermute | solution.py:657
  6.7 5.5 %collective-permute-start = (f32[5,6,3,8,128]{4,3,2,1,0:T(8,128)S(1)}, f32[5,6,3,8,128]{4,3,2,1,0:T(8,128)S(1)}, u32[]{:S(2)}, u32[]{:S(2)}) collective-permute-start(f32[5,6,3,8,128]{4,3,2,1,0:T(8,128)S(1)} %get-tuple-element.115), channel_id=1, source_target_pairs={{0,1},{1,0},{2,3},{3,2},{4,5},{5,4},{6,7},{7,6},{8,9},{9,8},{10,11... | collective-permute-start | bytes 1105928 | tf_op jit(solution)/shard_map/cond/branch_0_fun/ppermute | solution.py:635
  7.7 9.2 %collective-permute-start.1 = (f32[5,6,3,8,128]{4,3,2,1,0:T(8,128)S(1)}, f32[5,6,3,8,128]{4,3,2,1,0:T(8,128)S(1)}, u32[]{:S(2)}, u32[]{:S(2)}) collective-permute-start(f32[5,6,3,8,128]{4,3,2,1,0:T(8,128)S(1)} %get-tuple-element.116), channel_id=1, source_target_pairs={{1,2},{2,1},{5,6},{6,5},{9,10},{10,9},{13,14},{14,13},{17,18},{18,... | collective-permute-start | bytes 1105928 | tf_op jit(solution)/shard_map/cond/branch_0_fun/ppermute | solution.py:636
  10.7 22.7 %collective-permute-start.3 = (f32[5,3,32,128]{3,2,1,0:T(8,128)S(1)}, f32[5,3,32,128]{3,2,1,0:T(8,128)}, u32[]{:S(2)}, u32[]{:S(2)}) collective-permute-start(f32[5,3,32,128]{3,2,1,0:T(8,128)S(1)} %get-tuple-element.121), channel_id=1, source_target_pairs={{0,20},{4,16},{8,28},{12,24},{16,4},{20,0},{24,12},{28,8},{1,21},{... | collective-permute-start | bytes 737288 | tf_op jit(solution)/shard_map/cond/branch_0_fun/ppermute | solution.py:658
  10.8 22.6 %collective-permute-start.4 = (f32[5,8,128]{2,1,0:T(8,128)S(1)}, f32[5,8,128]{2,1,0:T(8,128)}, u32[]{:S(2)}, u32[]{:S(2)}) collective-permute-start(f32[5,8,128]{2,1,0:T(8,128)S(1)} %get-tuple-element.122), channel_id=1, source_target_pairs={{0,4},{4,0},{8,12},{12,8},{1,5},{5,1},{9,13},{13,9},{2,6},{6,2},{1... | collective-permute-start | bytes 61448 | tf_op jit(solution)/shard_map/cond/branch_0_fun/ppermute | solution.py:637
  12.2 21.2 %collective-permute-start.5 = (f32[5,8,128]{2,1,0:T(8,128)S(1)}, f32[5,8,128]{2,1,0:T(8,128)}, u32[]{:S(2)}, u32[]{:S(2)}) collective-permute-start(f32[5,8,128]{2,1,0:T(8,128)S(1)} %get-tuple-element.123), channel_id=1, source_target_pairs={{4,8},{8,4},{12,0},{0,12},{5,9},{9,5},{13,1},{1,13},{6,10},{10,6},... | collective-permute-start | bytes 61448 | tf_op jit(solution)/shard_map/cond/branch_0_fun/ppermute | solution.py:638

commit v5 on v4

--- a/solution.py
+++ b/solution.py
@@ -73,7 +73,7 @@
 
 
 def face_terms(diff_state, diff_flux, sum_state, sum_flux, wave):
-    inv = inverse(sum_state(0))
+    inv = pl.reciprocal(sum_state(0), approx=True)
     un, va, vb, specific = (inv * sum_state(k) for k in range(1, 5))
     half = 0.5 * (un * un + va * va + vb * vb)
     internal = specific - half

time: 39.9 us -> 40.2 us (level)
  the two profiles are of different devices: /device:TPU:9 before, /device:TPU:1 now
where the time goes in v5:
time: 40.2 us; the launch traced here: 40.4 us
  Pallas kernels  24.1 us (60%)
  starting transfers between devices  10.9 us (27%)
  waiting for transfers between devices  3.4 us (8%)
  local copies, waits for them, and re-layouts  1.2 us (3%)
  between operations  0.71 us (2%)
    pallas_call x1, Pallas kernels, inner(): pl.pallas_call(functools.partial(inner_kernel, bands), in_specs=[vmem] *...  16.4 us
    pallas_call x1, Pallas kernels, tail(): pl.pallas_call(functools.partial(tail_kernel, gathered), in_specs=[smem,...  6.23 us
    ppermute x1, starting transfers between devices, run(): whole = lax.ppermute(whole, ('blk', 'theta'), whole_route)  4.13 us
    ppermute x1, waiting for transfers between devices, halos(): lax.ppermute(odd_radial, 'radial', pairs(parts, 1, False))  3.39 us
    ppermute x1, starting transfers between devices, halos(): lax.ppermute(odd_radial, 'radial', pairs(parts, 1, False))  3.03 us
    pallas_call x1, Pallas kernels, pack(): pl.pallas_call(functools.partial(pack_kernel, bands), in_specs=[smem, vme...  1.49 us
    ppermute x1, starting transfers between devices, halos(): lax.ppermute(even_theta, 'theta', pairs(slabs, 0, True))  1.42 us
    ppermute x1, starting transfers between devices, halos(): lax.ppermute(odd_theta, 'theta', pairs(slabs, 1, True))  1.29 us
  transfers between devices with their start and end apart: 6, of which 1 were waited for; matrix products, arithmetic and copies ran while one was open for 0% of the time, Pallas kernels for 41%

profile of v5, /device:TPU:1, one launch (start us, length us, event | category | flops | bytes accessed | tf_op | source)
XLA Modules:
  0.0 40.4 jit_solution(8423632544055870034)
XLA Ops:
  0.7 0.0 copy-start
  0.7 1.2 %copy-done = f32[5,6,8,1024]{3,2,1,0:T(8,128)S(1)} copy-done((f32[5,6,8,1024]{3,2,1,0:T(8,128)S(1)}, f32[5,6,8,1024]{3,2,1,0:T(8,128)}, u32[]{:S(2)}) %copy-start) | copy-done | bytes 983064
  1.9 1.5 %pack.1 = (f32[5,6,64,128]{3,2,1,0:T(8,128)S(1)}, f32[5,8,128]{2,1,0:T(8,128)S(1)}, f32[5,8,128]{2,1,0:T(8,128)S(1)}, f32[5,8,128]{2,1,0:T(8,128)S(1)}, f32[5,6,...) custom-call(s32[1]{0:T(128)} %copy.40.rotor_step, ...), custom_call_target="tpu_custom_call" | custom-call | tf_op jit(solution)/shard_map/pack/pallas_call | solution.py:269
  3.4 0.0 copy-start.1
  3.4 30.8 %conditional.1 = (f32[5,8,64,128]{3,2,1,0:T(8,128)S(1)}, bf16[480,1024]{1,0:T(8,128)(2,1)S(1)}, f32[5,3,64,128]{3,2,1,0:T(8,128)}, f32[5,3,32,128]{3,2,1,0:T(8,1...) conditional(s32[]{:T(128)} %clamp.3, (f32[5,6,3,8,128]{4,3,2,1,0:T(8,128)S(1)}, ...), branch_computations={%region_0.0_spmd, %region_1.0_spmd, %region_2.0_spmd, %region_3.0_... | conditional | flops 117555200 | bytes 9994528 | solution.py:668
  3.4 4.1 %collective-permute-start.20 = (f32[5,3,64,128]{3,2,1,0:T(8,128)S(1)}, f32[5,3,64,128]{3,2,1,0:T(8,128)}, u32[]{:S(2)}, u32[]{:S(2)}) collective-permute-start(f32[5,3,64,128]{3,2,1,0:T(8,128)S(1)} %get-tuple-element.153), channel_id=1, source_target_pairs={{0,24},{4,20},{8,16},{12,28},{16,8},{20,4},{24,0},{28,12},{1,25},{... | collective-permute-start | bytes 1474568 | tf_op jit(solution)/shard_map/cond/branch_3_fun/ppermute | solution.py:657
  7.5 1.0 %collective-permute-start.18 = (f32[5,6,3,8,128]{4,3,2,1,0:T(8,128)S(1)}, f32[5,6,3,8,128]{4,3,2,1,0:T(8,128)S(1)}, u32[]{:S(2)}, u32[]{:S(2)}) collective-permute-start(f32[5,6,3,8,128]{4,3,2,1,0:T(8,128)S(1)} %get-tuple-element.148), channel_id=1, source_target_pairs={{0,1},{1,0},{2,3},{3,2},{4,5},{5,4},{6,7},{7,6},{8,9},{9,8},{10,11... | collective-permute-start | bytes 1105928 | tf_op jit(solution)/shard_map/cond/branch_3_fun/ppermute | solution.py:635
  8.5 3.0 %collective-permute-start.19 = (f32[5,6,3,8,128]{4,3,2,1,0:T(8,128)S(1)}, f32[5,6,3,8,128]{4,3,2,1,0:T(8,128)S(1)}, u32[]{:S(2)}, u32[]{:S(2)}) collective-permute-start(f32[5,6,3,8,128]{4,3,2,1,0:T(8,128)S(1)} %get-tuple-element.149), channel_id=1, source_target_pairs={{1,2},{2,1},{5,6},{6,5},{9,10},{10,9},{13,14},{14,13},{17,18},{18,... | collective-permute-start | bytes 1105928 | tf_op jit(solution)/shard_map/cond/branch_3_fun/ppermute | solution.py:636
  11.5 0.1 collective-permute-start.21
  11.6 1.4 %collective-permute-start.22 = (f32[5,8,128]{2,1,0:T(8,128)S(1)}, f32[5,8,128]{2,1,0:T(8,128)}, u32[]{:S(2)}, u32[]{:S(2)}) collective-permute-start(f32[5,8,128]{2,1,0:T(8,128)S(1)} %get-tuple-element.155), channel_id=1, source_target_pairs={{0,4},{4,0},{8,12},{12,8},{1,5},{5,1},{9,13},{13,9},{2,6},{6,2},{1... | collective-permute-start | bytes 61448 | tf_op jit(solution)/shard_map/cond/branch_3_fun/ppermute | solution.py:637
  13.0 0.0 collective-permute-done.18.even_radial
  13.0 1.3 %collective-permute-start.23 = (f32[5,8,128]{2,1,0:T(8,128)S(1)}, f32[5,8,128]{2,1,0:T(8,128)}, u32[]{:S(2)}, u32[]{:S(2)}) collective-permute-start(f32[5,8,128]{2,1,0:T(8,128)S(1)} %get-tuple-element.156), channel_id=1, source_target_pairs={{4,8},{8,4},{12,0},{0,12},{5,9},{9,5},{13,1},{1,13},{6,10},{10,6},... | collective-permute-start | bytes 61448 | tf_op jit(solution)/shard_map/cond/branch_3_fun/ppermute | solution.py:638
  14.3 3.4 %collective-permute-done.19.odd_radial = f32[5,6,3,8,128]{4,3,2,1,0:T(8,128)S(1)} collective-permute-done((f32[5,6,3,8,128]{4,3,2,1,0:T(8,128)S(1)}, f32[5,6,3,8,128]{4,3,2,1,0:T(8,128)S(1)}, u32[]{:S(2)}, u32[]{:S(2)}) %collective-permute-start.19) | collective-permute-done | bytes 368672 | tf_op jit(solution)/shard_map/cond/branch_3_fun/ppermute | solution.py:636
  17.7 16.4 %inner.9 = (f32[5,8,64,128]{3,2,1,0:T(8,128)S(1)}, bf16[480,1024]{1,0:T(8,128)(2,1)S(1)}) custom-call(f32[5,6,64,128]{3,2,1,0:T(8,128)S(1)} %get-tuple-element.146.section, f32[5,8,6,8,128]{4,3,2,1,0:T(8,128)S(1)} %get-tuple-element.147.cells, f32[5,6,3,8,128]{4,3,2,1,0:T(8,128)S(1)} %collective-permute-done.18.even_radial, ...), custom_call_target="tpu_custom_call" | custom-call | flops 117555200 | bytes 3932160 | tf_op jit(solution)/shard_map/cond/branch_3_fun/inner/pallas_call | solution.py:448
  34.1 0.0 collective-permute-done.22
  34.2 0.0 collective-permute-done.23
  34.2 0.0 collective-permute-done.21
  34.2 0.0 collective-permute-done.20
  34.2 0.0 copy-done.1
  34.2 6.2 %tail.1 = f32[5,6,64,128]{3,2,1,0:T(8,128)} custom-call(s32[1]{0:T(128)} %copy.40.rotor_step, f32[5,6,64,128]{3,2,1,0:T(8,128)S(1)} %bitcast.20, f32[5,8,64,128]{3,2,1,0:T(8,128)S(1)} %get-tuple-element.203.acc, bf16[480,1024]{1,0:T(8,128)(2,1)S(1)} %get-tuple-element.204.split, bf16[1024,1024]{1,0:T(8,128)(2,1)S(1)} %get-tuple-element.205.order, ...), custom_call_target="tpu_custom_call" | custom-call | tf_op jit(solution)/shard_map/tail/pallas_call | solution.py:583
Async XLA Ops:
  0.7 1.2 %copy-start = (f32[5,6,8,1024]{3,2,1,0:T(8,128)S(1)}, f32[5,6,8,1024]{3,2,1,0:T(8,128)}, u32[]{:S(2)}) copy-start(f32[5,6,8,1024]{3,2,1,0:T(8,128)} %param.10) | copy-start | bytes 2949124
  3.4 30.8 %copy-start.1 = (f32[5,6,8,1024]{3,2,1,0:T(8,128)S(1)}, f32[5,6,8,1024]{3,2,1,0:T(8,128)}, u32[]{:S(2)}) copy-start(f32[5,6,8,1024]{3,2,1,0:T(8,128)} %param.10) | copy-start | bytes 2949124
  3.4 30.8 %collective-permute-start.20 = (f32[5,3,64,128]{3,2,1,0:T(8,128)S(1)}, f32[5,3,64,128]{3,2,1,0:T(8,128)}, u32[]{:S(2)}, u32[]{:S(2)}) collective-permute-start(f32[5,3,64,128]{3,2,1,0:T(8,128)S(1)} %get-tuple-element.153), channel_id=1, source_target_pairs={{0,24},{4,20},{8,16},{12,28},{16,8},{20,4},{24,0},{28,12},{1,25},{... | collective-permute-start | bytes 1474568 | tf_op jit(solution)/shard_map/cond/branch_3_fun/ppermute | solution.py:657
  7.5 5.5 %collective-permute-start.18 = (f32[5,6,3,8,128]{4,3,2,1,0:T(8,128)S(1)}, f32[5,6,3,8,128]{4,3,2,1,0:T(8,128)S(1)}, u32[]{:S(2)}, u32[]{:S(2)}) collective-permute-start(f32[5,6,3,8,128]{4,3,2,1,0:T(8,128)S(1)} %get-tuple-element.148), channel_id=1, source_target_pairs={{0,1},{1,0},{2,3},{3,2},{4,5},{5,4},{6,7},{7,6},{8,9},{9,8},{10,11... | collective-permute-start | bytes 1105928 | tf_op jit(solution)/shard_map/cond/branch_3_fun/ppermute | solution.py:635
  8.5 9.2 %collective-permute-start.19 = (f32[5,6,3,8,128]{4,3,2,1,0:T(8,128)S(1)}, f32[5,6,3,8,128]{4,3,2,1,0:T(8,128)S(1)}, u32[]{:S(2)}, u32[]{:S(2)}) collective-permute-start(f32[5,6,3,8,128]{4,3,2,1,0:T(8,128)S(1)} %get-tuple-element.149), channel_id=1, source_target_pairs={{1,2},{2,1},{5,6},{6,5},{9,10},{10,9},{13,14},{14,13},{17,18},{18,... | collective-permute-start | bytes 1105928 | tf_op jit(solution)/shard_map/cond/branch_3_fun/ppermute | solution.py:636
  11.5 22.6 %collective-permute-start.21 = (f32[5,3,32,128]{3,2,1,0:T(8,128)S(1)}, f32[5,3,32,128]{3,2,1,0:T(8,128)}, u32[]{:S(2)}, u32[]{:S(2)}) collective-permute-start(f32[5,3,32,128]{3,2,1,0:T(8,128)S(1)} %get-tuple-element.154), channel_id=1, source_target_pairs={{0,20},{4,16},{8,28},{12,24},{16,4},{20,0},{24,12},{28,8},{1,21},{... | collective-permute-start | bytes 737288 | tf_op jit(solution)/shard_map/cond/branch_3_fun/ppermute | solution.py:658
  11.6 22.5 %collective-permute-start.22 = (f32[5,8,128]{2,1,0:T(8,128)S(1)}, f32[5,8,128]{2,1,0:T(8,128)}, u32[]{:S(2)}, u32[]{:S(2)}) collective-permute-start(f32[5,8,128]{2,1,0:T(8,128)S(1)} %get-tuple-element.155), channel_id=1, source_target_pairs={{0,4},{4,0},{8,12},{12,8},{1,5},{5,1},{9,13},{13,9},{2,6},{6,2},{1... | collective-permute-start | bytes 61448 | tf_op jit(solution)/shard_map/cond/branch_3_fun/ppermute | solution.py:637
  13.0 21.1 %collective-permute-start.23 = (f32[5,8,128]{2,1,0:T(8,128)S(1)}, f32[5,8,128]{2,1,0:T(8,128)}, u32[]{:S(2)}, u32[]{:S(2)}) collective-permute-start(f32[5,8,128]{2,1,0:T(8,128)S(1)} %get-tuple-element.156), channel_id=1, source_target_pairs={{4,8},{8,4},{12,0},{0,12},{5,9},{9,5},{13,1},{1,13},{6,10},{10,6},... | collective-permute-start | bytes 61448 | tf_op jit(solution)/shard_map/cond/branch_3_fun/ppermute | solution.py:638
